TPU v7x, 128 devices: a whole 4x4x4 slice. The times are simulated.
128 devices in a mesh: dp: 8 (over x, core), list: 16 (over y, z).
Axes of the slice: x: 4, y: 4, z: 4, core: 2. Of those that a mesh axis runs over, the one named last changes fastest.
Arguments:
- vectors: bfloat16 [262144, 768], P(('dp', 'list')), may hold values from -6 to 6
- list_ids: int32 [262144], P(('dp', 'list')), may hold values from 0 to 4095
- codes: int32 [262144, 96], P(('dp', 'list')), may hold values from 0 to 255
- fill_counts: int32 [128, 16], P(('dp', 'list')), may hold values from 1 to 128, as said below
- centroids: bfloat16 [65536, 768], P('list'), may hold values from -6 to 6
- codebooks: float32 [96, 8, 256], replicated, may hold values from -4 to 4
Outputs:
- quant_error: bfloat16 [262144, 768], P(('dp', 'list'))
- new_codebooks: float32 [96, 8, 256], replicated
- gram: float32 [768, 768], replicated
Inputs may be any that keep to these rules, and one draw needn't show every extreme that they name: `fill_counts`: every entry is at least 1 and at most 128; in every draw some owner has 128 used slots in the block of every device.
All inputs are finite; a program needn't handle non-finite values.
Results may differ from a plain program's by a relative error of at most 0.0051.
Values may be sent and summed in bfloat16 or wider, within the bound.
A program may use at most 128 MiB of HBM per device.

v0:
```python
import jax
import jax.numpy as jnp
from jax import lax
from jax.sharding import PartitionSpec as P


def local(vectors, list_ids, codes, fill_counts, centroids, codebooks):
    owners = lax.axis_size("list")
    slots = vectors.shape[0]
    width = vectors.shape[1]
    cap = slots // owners
    subspaces = codes.shape[1]
    subwidth = width // subspaces
    words = codebooks.shape[2]
    blocks = vectors.reshape(owners, cap, width)
    id_blocks = list_ids.reshape(owners, cap)
    arrived = lax.all_to_all(blocks, "list", split_axis=0, concat_axis=0, tiled=True)
    wanted = lax.all_to_all(id_blocks, "list", split_axis=0, concat_axis=0, tiled=True)
    rows = jnp.take(centroids, wanted, axis=0)
    diff = (arrived.astype(jnp.float32) - rows.astype(jnp.float32)).astype(jnp.bfloat16)
    residual = lax.all_to_all(diff, "list", split_axis=0, concat_axis=0, tiled=True)
    live = (jnp.arange(cap, dtype=jnp.int32)[None, :] < fill_counts[0][:, None]).astype(
        jnp.bfloat16
    )
    residual = (residual * live[:, :, None]).reshape(slots, width)
    live_rows = live.reshape(slots)
    gram_part = jnp.dot(residual.T, residual, preferred_element_type=jnp.float32)
    step_rows = min(256, slots)
    turns = slots // step_rows
    kinds = jnp.arange(words, dtype=jnp.int32)
    res_steps = residual.reshape(turns, step_rows, width)
    code_steps = codes.reshape(turns, step_rows, subspaces)
    live_steps = live_rows.reshape(turns, step_rows)

    def accumulate(carry, pieces_in):
        sums, counts = carry
        res_part, code_part, live_part = pieces_in
        onehot = (code_part[:, :, None] == kinds).astype(jnp.bfloat16) * live_part[:, None, None]
        sums = sums + jnp.einsum(
            "rmd,rmk->mdk",
            res_part.reshape(step_rows, subspaces, subwidth),
            onehot,
            preferred_element_type=jnp.float32,
        )
        counts = counts + jnp.sum(onehot.astype(jnp.float32), axis=0)
        return ((sums, counts), None)

    start_carry = (
        jnp.zeros((subspaces, subwidth, words), jnp.float32),
        jnp.zeros((subspaces, words), jnp.float32),
    )
    (sums, counts), unused = lax.scan(accumulate, start_carry, (res_steps, code_steps, live_steps))
    gram_reduced, sums, counts = lax.psum((gram_part, sums, counts), ("dp", "list"))
    new_books = (sums + codebooks) / (counts[:, None, :] + 1.0)

    def reconstruct(carry, pieces_in):
        res_part, code_part, live_part = pieces_in
        onehot = (code_part[:, :, None] == kinds).astype(jnp.float32)
        recon = jnp.einsum(
            "rmk,mdk->rmd", onehot, new_books, precision=lax.Precision.HIGHEST
        ).reshape(step_rows, width)
        error = (res_part.astype(jnp.float32) - recon) * live_part.astype(jnp.float32)[:, None]
        return (carry, error.astype(jnp.bfloat16))

    unused, errors = lax.scan(reconstruct, 0, (res_steps, code_steps, live_steps))
    total_rows = float(slots * lax.axis_size("dp") * owners)
    return (errors.reshape(slots, width), new_books, gram_reduced / total_rows)


def solution(mesh):
    in_specs = (
        P(("dp", "list"), None),
        P(("dp", "list")),
        P(("dp", "list"), None),
        P(("dp", "list"), None),
        P("list", None),
        P(),
    )
    out_specs = (P(("dp", "list"), None), P(), P())
    return jax.shard_map(local, mesh=mesh, in_specs=in_specs, out_specs=out_specs, check_vma=False)
```

profile of v0, /device:TPU:1, one launch (start us, length us, event | category | flops | bytes accessed | tf_op | source)
XLA Modules:
  0.0 517.8 jit_solution(384444589883736717)
XLA Ops:
  7.2 14.9 %all_to_all.25 = s32[16,1,128]{2,1,0:T(1,128)S(1)} all-to-all(s32[16,1,128]{2,1,0:T(1,128)} %bitcast.65), channel_id=1, replica_groups=mesh['dp'=8,'list'=16] {'list'}, dimensions={0} | all-to-all | bytes 16384 | tf_op jit(solution)/shard_map/all_to_all | solution.py:18
  25.9 13.7 %gather_fusion = bf16[2048,768]{1,0:T(8,128)(2,1)} fusion(bf16[4096,768]{1,0:T(8,128)(2,1)} %param.14, s32[2048]{0:T(1024)S(1)} %fusion.25), kind=kCustom, calls=%fused_computation | custom fusion | bytes 6299648 | tf_op jit(solution)/shard_map/jit(_take)/gather | solution.py:19
  39.5 23.2 %all-to-all-done = bf16[16,128,768]{2,1,0:T(8,128)(2,1)S(1)} async-done(((bf16[16,128,768]{2,1,0:T(8,128)(2,1)}), bf16[16,128,768]{2,1,0:T(8,128)(2,1)S(1)}, u32[]{:S(2)}, u32[]{:S(2)}) %all-to-all-start) | async-done | bytes 3145760 | tf_op jit(solution)/shard_map/all_to_all | solution.py:17
  66.4 6.3 %all-to-all-start.2 = ((bf16[16,128,768]{2,1,0:T(8,128)(2,1)}), bf16[16,128,768]{2,1,0:T(8,128)(2,1)S(1)}, u32[]{:S(2)}, u32[]{:S(2)}) async-start(bf16[16,128,768]{2,1,0:T(8,128)(2,1)} %subtract_convert_fusion), calls=%async_computation.2 | async-start | bytes 6291456 | tf_op jit(solution)/shard_map/all_to_all | solution.py:21
  76.5 32.4 %all-to-all-done.2 = bf16[16,128,768]{2,1,0:T(8,128)(2,1)S(1)} async-done(((bf16[16,128,768]{2,1,0:T(8,128)(2,1)}), bf16[16,128,768]{2,1,0:T(8,128)(2,1)S(1)}, u32[]{:S(2)}, u32[]{:S(2)}) %all-to-all-start.2) | async-done | bytes 3145760 | tf_op jit(solution)/shard_map/all_to_all | solution.py:21
  113.4 4.7 copy.24
  118.2 109.0 %while.25 = (s32[]{:T(128)}, f32[96,8,256]{2,1,0:T(8,128)S(1)}, f32[96,256]{1,0:T(8,128)S(1)}, bf16[8,256,768]{1,2,0:T(8,128)(2,1)}, s32[8,256,96]{1,2,0:T(8,128...) while((s32[]{:T(128)}, f32[96,8,256]{2,1,0:T(8,128)S(1)}, f32[96,256]{1,0:T(8,128)S(1)}, ...), condition=%wide.region_2.3_spmd.clone, body=%wide.region_0.0_spmd.clone.sunk | while | flops 138829824 | bytes 2755176 | solution.py:52
  119.1 4.5 fusion.42
  123.5 8.2 %convert_reduce_fusion.2 = f32[96,256]{1,0:T(8,128)S(1)} fusion(s32[256,96]{0,1:T(8,128)S(1)} %dynamic-slice_bitcast_fusion.5, bf16[256]{0:T(256)(128)(2,1)S(1)} %dynamic-slice_reduce_fusion.2), kind=kLoop, calls=%fused_computation.15.clone.1 | loop fusion | flops 25141248 | bytes 197120 | tf_op jit(solution)/shard_map/while/body/eval_jaxpr/reduce_sum | solution.py:45
  132.7 4.5 fusion.42
  137.2 8.2 %convert_reduce_fusion.2 = f32[96,256]{1,0:T(8,128)S(1)} fusion(s32[256,96]{0,1:T(8,128)S(1)} %dynamic-slice_bitcast_fusion.5, bf16[256]{0:T(256)(128)(2,1)S(1)} %dynamic-slice_reduce_fusion.2), kind=kLoop, calls=%fused_computation.15.clone.1 | loop fusion | flops 25141248 | bytes 197120 | tf_op jit(solution)/shard_map/while/body/eval_jaxpr/reduce_sum | solution.py:45
  146.3 4.5 fusion.42
  150.8 8.2 %convert_reduce_fusion.2 = f32[96,256]{1,0:T(8,128)S(1)} fusion(s32[256,96]{0,1:T(8,128)S(1)} %dynamic-slice_bitcast_fusion.5, bf16[256]{0:T(256)(128)(2,1)S(1)} %dynamic-slice_reduce_fusion.2), kind=kLoop, calls=%fused_computation.15.clone.1 | loop fusion | flops 25141248 | bytes 197120 | tf_op jit(solution)/shard_map/while/body/eval_jaxpr/reduce_sum | solution.py:45
  159.9 4.5 fusion.42
  164.4 8.2 %convert_reduce_fusion.2 = f32[96,256]{1,0:T(8,128)S(1)} fusion(s32[256,96]{0,1:T(8,128)S(1)} %dynamic-slice_bitcast_fusion.5, bf16[256]{0:T(256)(128)(2,1)S(1)} %dynamic-slice_reduce_fusion.2), kind=kLoop, calls=%fused_computation.15.clone.1 | loop fusion | flops 25141248 | bytes 197120 | tf_op jit(solution)/shard_map/while/body/eval_jaxpr/reduce_sum | solution.py:45
  173.6 4.5 fusion.42
  178.0 8.2 %convert_reduce_fusion.2 = f32[96,256]{1,0:T(8,128)S(1)} fusion(s32[256,96]{0,1:T(8,128)S(1)} %dynamic-slice_bitcast_fusion.5, bf16[256]{0:T(256)(128)(2,1)S(1)} %dynamic-slice_reduce_fusion.2), kind=kLoop, calls=%fused_computation.15.clone.1 | loop fusion | flops 25141248 | bytes 197120 | tf_op jit(solution)/shard_map/while/body/eval_jaxpr/reduce_sum | solution.py:45
  187.2 4.5 fusion.42
  191.7 8.2 %convert_reduce_fusion.2 = f32[96,256]{1,0:T(8,128)S(1)} fusion(s32[256,96]{0,1:T(8,128)S(1)} %dynamic-slice_bitcast_fusion.5, bf16[256]{0:T(256)(128)(2,1)S(1)} %dynamic-slice_reduce_fusion.2), kind=kLoop, calls=%fused_computation.15.clone.1 | loop fusion | flops 25141248 | bytes 197120 | tf_op jit(solution)/shard_map/while/body/eval_jaxpr/reduce_sum | solution.py:45
  200.8 4.5 fusion.42
  205.3 8.2 %convert_reduce_fusion.2 = f32[96,256]{1,0:T(8,128)S(1)} fusion(s32[256,96]{0,1:T(8,128)S(1)} %dynamic-slice_bitcast_fusion.5, bf16[256]{0:T(256)(128)(2,1)S(1)} %dynamic-slice_reduce_fusion.2), kind=kLoop, calls=%fused_computation.15.clone.1 | loop fusion | flops 25141248 | bytes 197120 | tf_op jit(solution)/shard_map/while/body/eval_jaxpr/reduce_sum | solution.py:45
  218.9 8.2 %convert_reduce_fusion.2 = f32[96,256]{1,0:T(8,128)S(1)} fusion(s32[256,96]{0,1:T(8,128)S(1)} %dynamic-slice_bitcast_fusion.5, bf16[256]{0:T(256)(128)(2,1)S(1)} %dynamic-slice_reduce_fusion.2), kind=kLoop, calls=%fused_computation.15.clone.1 | loop fusion | flops 25141248 | bytes 197120 | tf_op jit(solution)/shard_map/while/body/eval_jaxpr/reduce_sum | solution.py:45
  228.1 158.6 %all-reduce.3.cloned.1.call-done = (f32[96,8,256]{2,1,0:T(8,128)}, f32[96,256]{1,0:T(8,128)}, f32[768,768]{1,0:T(8,128)}) async-done(((f32[96,8,256]{2,1,0:T(8,128)}, f32[96,256]{1,0:T(8,128)}, f32[768,768]{1,0:T(8,128)}), (f32[96,8,256]{2,1,0:T(8,128)}, f32[96,256]{1,0:T(8,128)}, f32[768,768]{1,0:T(8,128)})) %all-reduce.3.cloned.1.call-update) | async-done | bytes 3244048 | tf_op jit(solution)/shard_map/psum | solution.py:53
  389.7 119.6 %while.24 = (s32[]{:T(128)}, bf16[8,256,768]{2,1,0:T(8,128)(2,1)}, bf16[8,256,768]{1,2,0:T(8,128)(2,1)}, s32[8,256,96]{1,2,0:T(8,128)}, f32[96,8,256]{2,1,0:T(8,128)}, /*index=5*/bf16[8,256]{1,0:T(8,128)(2,1)S(1)}, s32[]{:T(128)}) while((s32[]{:T(128)}, bf16[8,256,768]{2,1,0:T(8,128)(2,1)}, bf16[8,256,768]{1,2,0:T(8,128)(2,1)}, ...), condition=%wide.region_6.7_spmd.clone, body=%wide.region_5.6_spmd.clone.sunk | while | flops 611057920 | bytes 3443801 | solution.py:65
  390.8 13.1 %fusion.39 = bf16[1,256,768]{1,2,0:T(8,128)(2,1)S(1)} fusion(f32[96,8,256]{2,1,0:T(8,128)} %get-tuple-element.285, s32[256,96]{0,1:T(8,128)S(1)} %dynamic-slice_bitcast_fusion.4, f32[256]{0:T(256)S(1)} %bitcast.64, bf16[8,256,768]{1,2,0:T(8,128)(2,1)} %get-tuple-element.283, s32[]{:T(128)} %get-tuple-element.274), kind=kOutput, calls=%fused_computation.9.clone.1 | convolution fusion | flops 611057664 | bytes 1672196 | tf_op jit(solution)/shard_map/while/body/eval_jaxpr/rmk,mdk->rmd/dot_general | solution.py:59
  405.7 13.1 %fusion.39 = bf16[1,256,768]{1,2,0:T(8,128)(2,1)S(1)} fusion(f32[96,8,256]{2,1,0:T(8,128)} %get-tuple-element.285, s32[256,96]{0,1:T(8,128)S(1)} %dynamic-slice_bitcast_fusion.4, f32[256]{0:T(256)S(1)} %bitcast.64, bf16[8,256,768]{1,2,0:T(8,128)(2,1)} %get-tuple-element.283, s32[]{:T(128)} %get-tuple-element.274), kind=kOutput, calls=%fused_computation.9.clone.1 | convolution fusion | flops 611057664 | bytes 1672196 | tf_op jit(solution)/shard_map/while/body/eval_jaxpr/rmk,mdk->rmd/dot_general | solution.py:59
  420.7 13.1 %fusion.39 = bf16[1,256,768]{1,2,0:T(8,128)(2,1)S(1)} fusion(f32[96,8,256]{2,1,0:T(8,128)} %get-tuple-element.285, s32[256,96]{0,1:T(8,128)S(1)} %dynamic-slice_bitcast_fusion.4, f32[256]{0:T(256)S(1)} %bitcast.64, bf16[8,256,768]{1,2,0:T(8,128)(2,1)} %get-tuple-element.283, s32[]{:T(128)} %get-tuple-element.274), kind=kOutput, calls=%fused_computation.9.clone.1 | convolution fusion | flops 611057664 | bytes 1672196 | tf_op jit(solution)/shard_map/while/body/eval_jaxpr/rmk,mdk->rmd/dot_general | solution.py:59
  435.6 13.1 %fusion.39 = bf16[1,256,768]{1,2,0:T(8,128)(2,1)S(1)} fusion(f32[96,8,256]{2,1,0:T(8,128)} %get-tuple-element.285, s32[256,96]{0,1:T(8,128)S(1)} %dynamic-slice_bitcast_fusion.4, f32[256]{0:T(256)S(1)} %bitcast.64, bf16[8,256,768]{1,2,0:T(8,128)(2,1)} %get-tuple-element.283, s32[]{:T(128)} %get-tuple-element.274), kind=kOutput, calls=%fused_computation.9.clone.1 | convolution fusion | flops 611057664 | bytes 1672196 | tf_op jit(solution)/shard_map/while/body/eval_jaxpr/rmk,mdk->rmd/dot_general | solution.py:59
  450.5 13.1 %fusion.39 = bf16[1,256,768]{1,2,0:T(8,128)(2,1)S(1)} fusion(f32[96,8,256]{2,1,0:T(8,128)} %get-tuple-element.285, s32[256,96]{0,1:T(8,128)S(1)} %dynamic-slice_bitcast_fusion.4, f32[256]{0:T(256)S(1)} %bitcast.64, bf16[8,256,768]{1,2,0:T(8,128)(2,1)} %get-tuple-element.283, s32[]{:T(128)} %get-tuple-element.274), kind=kOutput, calls=%fused_computation.9.clone.1 | convolution fusion | flops 611057664 | bytes 1672196 | tf_op jit(solution)/shard_map/while/body/eval_jaxpr/rmk,mdk->rmd/dot_general | solution.py:59
  465.5 13.1 %fusion.39 = bf16[1,256,768]{1,2,0:T(8,128)(2,1)S(1)} fusion(f32[96,8,256]{2,1,0:T(8,128)} %get-tuple-element.285, s32[256,96]{0,1:T(8,128)S(1)} %dynamic-slice_bitcast_fusion.4, f32[256]{0:T(256)S(1)} %bitcast.64, bf16[8,256,768]{1,2,0:T(8,128)(2,1)} %get-tuple-element.283, s32[]{:T(128)} %get-tuple-element.274), kind=kOutput, calls=%fused_computation.9.clone.1 | convolution fusion | flops 611057664 | bytes 1672196 | tf_op jit(solution)/shard_map/while/body/eval_jaxpr/rmk,mdk->rmd/dot_general | solution.py:59
  480.4 13.1 %fusion.39 = bf16[1,256,768]{1,2,0:T(8,128)(2,1)S(1)} fusion(f32[96,8,256]{2,1,0:T(8,128)} %get-tuple-element.285, s32[256,96]{0,1:T(8,128)S(1)} %dynamic-slice_bitcast_fusion.4, f32[256]{0:T(256)S(1)} %bitcast.64, bf16[8,256,768]{1,2,0:T(8,128)(2,1)} %get-tuple-element.283, s32[]{:T(128)} %get-tuple-element.274), kind=kOutput, calls=%fused_computation.9.clone.1 | convolution fusion | flops 611057664 | bytes 1672196 | tf_op jit(solution)/shard_map/while/body/eval_jaxpr/rmk,mdk->rmd/dot_general | solution.py:59
  495.4 13.1 %fusion.39 = bf16[1,256,768]{1,2,0:T(8,128)(2,1)S(1)} fusion(f32[96,8,256]{2,1,0:T(8,128)} %get-tuple-element.285, s32[256,96]{0,1:T(8,128)S(1)} %dynamic-slice_bitcast_fusion.4, f32[256]{0:T(256)S(1)} %bitcast.64, bf16[8,256,768]{1,2,0:T(8,128)(2,1)} %get-tuple-element.283, s32[]{:T(128)} %get-tuple-element.274), kind=kOutput, calls=%fused_computation.9.clone.1 | convolution fusion | flops 611057664 | bytes 1672196 | tf_op jit(solution)/shard_map/while/body/eval_jaxpr/rmk,mdk->rmd/dot_general | solution.py:59
  (93 shorter events, 48.3 us)
Async XLA Ops:
  22.1 40.6 %all-to-all-start = ((bf16[16,128,768]{2,1,0:T(8,128)(2,1)}), bf16[16,128,768]{2,1,0:T(8,128)(2,1)S(1)}, u32[]{:S(2)}, u32[]{:S(2)}) async-start(bf16[16,128,768]{2,1,0:T(8,128)(2,1)} %bitcast.60), calls=%async_computation | async-start | bytes 6291456 | tf_op jit(solution)/shard_map/all_to_all | solution.py:17
  66.4 7.1 %copy-start.6 = (s32[1,16]{1,0:T(1,128)S(1)}, s32[1,16]{1,0:T(1,128)}, u32[]{:S(2)}) copy-start(s32[1,16]{1,0:T(1,128)} %param.13) | copy-start | bytes 196
  66.4 42.6 %all-to-all-start.2 = ((bf16[16,128,768]{2,1,0:T(8,128)(2,1)}), bf16[16,128,768]{2,1,0:T(8,128)(2,1)S(1)}, u32[]{:S(2)}, u32[]{:S(2)}) async-start(bf16[16,128,768]{2,1,0:T(8,128)(2,1)} %subtract_convert_fusion), calls=%async_computation.2 | async-start | bytes 6291456 | tf_op jit(solution)/shard_map/all_to_all | solution.py:21
  72.7 314.0 %all-reduce.3.cloned.1.call-start = ((), (), s32[]{:S(2)}) async-start(), calls=%async_computation.3 | async-start | bytes 6488064 | tf_op jit(solution)/shard_map/psum | solution.py:53
  109.3 4.1 copy-start
  113.4 4.7 copy-start.4
  227.1 0.6 copy-start.1
  227.1 0.9 copy-start.5
  227.2 160.4 %copy-start.3 = (f32[96,8,256]{2,1,0:T(8,128)S(1)}, f32[96,8,256]{2,1,0:T(8,128)}, u32[]{:S(2)}) copy-start(f32[96,8,256]{2,1,0:T(8,128)} %param.15) | copy-start | bytes 2359300
  389.7 119.7 %copy-start.2 = (f32[768,768]{1,0:T(8,128)S(1)}, f32[768,768]{1,0:T(8,128)}, u32[]{:S(2)}) copy-start(f32[768,768]{1,0:T(8,128)} %get-tuple-element.168) | copy-start | bytes 7077892
Sparse Core Ops, SparseCore 0:
  228.2 158.4 all-reduce.2
where the time goes:
time: 519 us; the launch traced here: 518 us
  waiting for transfers between devices  214 us (41%)
  matrix products  144 us (28%)
  other arithmetic  75.1 us (14%)
  local copies, waits for them, and re-layouts  44.4 us (9%)
  blocking collectives  14.9 us (3%)
  between operations  14.1 us (3%)
  starting transfers between devices  10.3 us (2%)
    psum x1, waiting for transfers between devices, local(): lax.psum((gram_part, sums, counts), ('dp', 'list'))  159 us
    dot_general x8, matrix products, reconstruct(): jnp.einsum('rmk,mdk->rmd', onehot, new_books, precision=lax.Precision.HIG...  105 us
    reduce_sum x8, other arithmetic, accumulate(): counts = counts + jnp.sum(onehot.astype(jnp.float32), axis=0)  65.4 us
    dot_general x8, matrix products, accumulate(): jnp.einsum('rmd,rmk->mdk', res_part.reshape(step_rows, subspaces, subwidt...  35.7 us
    all_to_all x1, waiting for transfers between devices, local(): lax.all_to_all(diff, 'list', split_axis=0, concat_axis=0, tiled=True)  32.4 us
    all_to_all x1, waiting for transfers between devices, local(): lax.all_to_all(blocks, 'list', split_axis=0, concat_axis=0, tiled=True)  23.2 us
    all_to_all x1, blocking collectives, local(): lax.all_to_all(id_blocks, 'list', split_axis=0, concat_axis=0, tiled=True)  14.9 us
    gather x1, local copies, waits for them, and re-layouts, local(): rows = jnp.take(centroids, wanted, axis=0)  13.7 us
  transfers between devices with their start and end apart: 3, of which 3 were waited for; matrix products, arithmetic and copies ran while one was open for 3% of the time, Pallas kernels for 0%

commit v1 on v0

v1 whole, which is shorter than its diff:
```python
import functools

import jax
import jax.numpy as jnp
from jax import lax
from jax.experimental import pallas as pl
from jax.experimental.pallas import tpu as pltpu
from jax.sharding import PartitionSpec as P

MESH = pl.DeviceIdType.MESH
F32 = jnp.float32
BF = jnp.bfloat16
NL, ND = 16, 8
CAP = 128
SLOTS = NL * CAP
NC = 6
CW = 128
MC = 16
GROUPS = ((0, 1, 2), (3, 4), (5,))
GSTEP = 512


def sum_rows(g):
    return len(GROUPS[g]) * 24


def block_of(j, i):
    return j * (j + 1) // 2 + i


def drain(ref, sem):
    pltpu.make_async_copy(ref, ref, sem).wait()


def refine_kernel(
    ids_ref, fill_ref, vec_hbm, codes_hbm, cent_hbm, books_hbm,
    rest_hbm, nb0_hbm, nb1_hbm, nb2_hbm, ga_hbm, gb_hbm,
    ids_in, ids_s, table, cbuf, gbuf, sbuf, rbuf, vec, codes, books, res, rest, live, acc,
    ds0, ds1, ds2, dr0, dr1, dr2, ls0, ls1, ls2, lr0, lr1, lr2,
    as0, as1, as2, ad0, ad1, ad2,
    gsa, gsb, gra, grb, gla, glb, gma, gmb, gta, gtb, gda, gdb,
    load_sem, cent_sem, out_sem, ids_ssem, ids_rsem, self_sem, x_ssem, x_rsem,
    ar_ssem, ar_rsem,
):
    dp = lax.axis_index("dp")
    me = lax.axis_index("list")
    my_y, my_z = me // 4, me % 4

    def list_peer(s):
        return lax.rem(my_y + s // 4, 4) * 4 + lax.rem(my_z + s % 4, 4)

    def dp_peer(s):
        return lax.rem(dp + s, ND)

    cent_rows = cbuf.shape[1]
    n_cent = cent_hbm.shape[0] // cent_rows

    def cent_copy(b):
        slot = lax.rem(b, 2)
        return pltpu.make_async_copy(
            cent_hbm.at[pl.ds(b * cent_rows, cent_rows)], cbuf.at[slot], cent_sem.at[slot])

    codes_load = pltpu.make_async_copy(codes_hbm, codes, load_sem.at[0])
    books_load = pltpu.make_async_copy(books_hbm, books, load_sem.at[1])
    vec_load = pltpu.make_async_copy(vec_hbm, vec, load_sem.at[2])
    cent_copy(0).start()
    cent_copy(1).start()

    barrier = pltpu.get_barrier_semaphore()

    def greet_list(s, c):
        pl.semaphore_signal(barrier, inc=1, device_id={"list": list_peer(s)}, device_id_type=MESH)
        return c

    def greet_dp(s, c):
        pl.semaphore_signal(barrier, inc=1, device_id={"dp": dp_peer(s)}, device_id_type=MESH)
        return c

    lax.fori_loop(1, NL, greet_list, 0)
    lax.fori_loop(1, ND, greet_dp, 0)
    pl.semaphore_wait(barrier, NL + ND - 2)

    def send_ids(s, c):
        p = list_peer(s)
        pltpu.make_async_remote_copy(
            src_ref=ids_ref.at[p], dst_ref=ids_in.at[me], send_sem=ids_ssem, recv_sem=ids_rsem,
            device_id={"list": p}, device_id_type=MESH).start()
        return c

    lax.fori_loop(1, NL, send_ids, 0)
    vec_load.start()
    codes_load.start()
    books_load.start()
    ids_in[me] = ids_ref[me]

    table_rows = table.reshape(4096 * 8, 128)
    gathered_rows = gbuf.reshape(CAP * 8, 128)

    def build(b, c):
        cent_copy(b).wait()
        slot = lax.rem(b, 2)

        def rows16(r, c):
            for j in range(NC):
                v = cbuf[slot, pl.ds(pl.multiple_of(r * 16, 16), 16), j * CW:(j + 1) * CW].astype(F32)
                base = (b * cent_rows + r * 16) * 8
                table_rows[pl.ds(base + j, 8, stride=8), :] = v[:8]
                table_rows[pl.ds(base + 64 + j, 8, stride=8), :] = v[8:]
            return c

        lax.fori_loop(0, cent_rows // 16, rows16, 0)

        @pl.when(b + 2 < n_cent)
        def _():
            cent_copy(b + 2).start()

        return c

    lax.fori_loop(0, n_cent, build, 0)

    drain(ids_in.at[pl.ds(0, NL - 1)], ids_rsem)
    drain(ids_in.at[pl.ds(0, NL - 1)], ids_ssem)
    to_smem = pltpu.make_async_copy(ids_in, ids_s, self_sem)
    to_smem.start()
    to_smem.wait()

    def x_copy(j, p):
        return pltpu.make_async_remote_copy(
            src_ref=sbuf.at[j, p], dst_ref=rbuf.at[j, me], send_sem=x_ssem, recv_sem=x_rsem.at[j],
            device_id={"list": p}, device_id_type=MESH)

    def gather(p):
        def rows(r, c):
            for k in range(16):
                at = r * 16 + k
                row = ids_s[p, 0, at]
                gbuf[at] = table[row]
            return c

        lax.fori_loop(0, CAP // 16, rows, 0)

        def pack(r, c):
            for j in range(NC):
                lo = gathered_rows[pl.ds(r * 128 + j, 8, stride=8), :]
                hi = gathered_rows[pl.ds(r * 128 + 64 + j, 8, stride=8), :]
                sbuf[j, p, pl.ds(pl.multiple_of(r * 16, 16), 16), :] = jnp.concatenate([lo, hi], 0).astype(BF)
            return c

        lax.fori_loop(0, CAP // 16, pack, 0)

    def gather_send(s, c):
        p = list_peer(s)
        gather(p)
        x_copy(0, p).start()
        return c

    lax.fori_loop(1, NL, gather_send, 0)

    def send_chunk(j, c):
        def one(s, c):
            x_copy(j, list_peer(s)).start()
            return c

        return lax.fori_loop(1, NL, one, c)

    lax.fori_loop(1, NC, send_chunk, 0)
    gather(me)

    def own(j, c):
        def rows(r, c):
            at = pl.ds(pl.multiple_of(r * 16, 16), 16)
            rbuf[j, me, at, :] = sbuf[j, me, at, :]
            return c

        return lax.fori_loop(0, CAP // 16, rows, c)

    lax.fori_loop(0, NC, own, 0)

    lane = lax.broadcasted_iota(jnp.int32, (16, CAP), 1)
    for p in range(NL):
        live[:, p * CAP:(p + 1) * CAP] = (lane < fill_ref[0, p]).astype(F32).astype(BF)

    vec_load.wait()
    codes_load.wait()
    books_load.wait()

    send_sums = (ds0, ds1, ds2)
    lane128 = lax.broadcasted_iota(jnp.int32, (8, 128), 1)
    row8 = lax.broadcasted_iota(jnp.int32, (8, 128), 0)
    sub16 = lax.broadcasted_iota(jnp.int32, (16, GSTEP), 0)
    sub16_f = sub16.astype(F32).astype(BF)
    sub16_h = (sub16 // 4).astype(F32).astype(BF)

    def residual_chunk(j):
        def one(p, c):
            rows = pl.ds(pl.multiple_of(p * CAP, CAP), CAP)
            v = vec[rows, pl.ds(pl.multiple_of(j * CW, CW), CW)].astype(F32)
            d = v - rbuf[j, p].astype(F32)
            keep = lax.broadcasted_iota(jnp.int32, (CAP, CW), 0) < fill_ref[0, p]
            d = jnp.where(keep, d, 0.0).astype(BF)
            res[j, rows, :] = d
            rest[j, :, pl.ds(pl.multiple_of(p * CAP, CAP), CAP)] = d.T
            return c

        lax.fori_loop(0, NL, one, 0)

    def hist_chunk(g, u, j):
        acc[...] = jnp.zeros_like(acc)

        def step(t, c):
            gs = pl.ds(pl.multiple_of(t * GSTEP, GSTEP), GSTEP)
            code = codes[j, :, gs]
            hi_all = (code >> 6).astype(F32)
            lo_all = (code & 63).astype(F32)
            alive = live[:, gs]
            zero = jnp.zeros((16, GSTEP), BF)
            one = jnp.ones((16, GSTEP), BF)
            for grp in range(4):
                left = []
                for pair in range(2):
                    m = grp * 4 + pair * 2
                    hi2 = jnp.concatenate([
                        jnp.broadcast_to(hi_all[m:m + 1], (8, GSTEP)),
                        jnp.broadcast_to(hi_all[m + 1:m + 2], (8, GSTEP))], 0).astype(BF)
                    r16 = rest[j, m * 8:m * 8 + 16, gs]
                    for h in range(4):
                        left.append(jnp.where(hi2 == jnp.array(h, BF), r16, zero))
                hi4 = hi_all[grp * 4:grp * 4 + 4]
                hi4 = jnp.concatenate([hi4, hi4, hi4, hi4], 0).astype(BF)
                left.append(jnp.where(hi4 == sub16_h, alive, zero))
                right = []
                for ml in range(4):
                    m = grp * 4 + ml
                    lo = jnp.broadcast_to(lo_all[m:m + 1], (16, GSTEP)).astype(BF)
                    for t16 in range(4):
                        right.append(jnp.where(lo == sub16_f + jnp.array(16 * t16, BF), one, zero))
                acc[grp] += lax.dot_general(
                    jnp.concatenate(left, 0), jnp.concatenate(right, 0),
                    (((1,), (1,)), ((), ())), preferred_element_type=F32)
            return c

        lax.fori_loop(0, SLOTS // GSTEP, step, 0)
        buf = send_sums[g]
        base = pl.multiple_of(u * 24, 8)
        for grp in range(4):
            for pair in range(2):
                q = grp * 2 + pair
                tile = slice(pair * 128, pair * 128 + 128)
                for t in range(2):
                    out = slice(t * 128, t * 128 + 128)
                    cnt = []
                    for m2 in range(2):
                        halves = []
                        for h, here in ((2 * t, m2 == 0), (2 * t + 1, m2 == 1)):
                            at = pair * 64 + h * 16 + m2 * 8
                            row = 128 + h * 4 + pair * 2 + m2
                            s = acc[grp, at:at + 8, tile]
                            n = jnp.broadcast_to(acc[grp, row:row + 1, tile], (8, 128))
                            if not here:
                                s = pltpu.roll(s, 64, 1)
                                n = pltpu.roll(n, 64, 1)
                            halves.append((s, n))
                        buf[q, pl.ds(base + m2 * 8, 8), out] = jnp.where(lane128 < 64, halves[0][0], halves[1][0])
                        cnt.append(jnp.where(lane128 < 64, halves[0][1], halves[1][1]))
                    buf[q, pl.ds(base + 16, 8), out] = jnp.where(row8 == 0, cnt[0], cnt[1])

    def gram_chunk(buf, j, first):
        def one(i, c):
            block = lax.dot_general(
                rest[j], res[i], (((1,), (0,)), ((), ())), preferred_element_type=F32) * (1.0 / (SLOTS * NL * ND))
            for q in range(ND):
                buf[q, first + i] = block[q * 16:q * 16 + 16].astype(BF)
            return c

        lax.fori_loop(0, j + 1, one, 0)

    def start_dp(a, src, dst):
        def one(s, c):
            q = dp_peer(s)
            pltpu.make_async_remote_copy(
                src_ref=src.at[q], dst_ref=dst.at[dp], send_sem=ar_ssem.at[a, 0], recv_sem=ar_rsem.at[a, 0],
                device_id={"dp": q}, device_id_type=MESH).start()
            return c

        lax.fori_loop(1, ND, one, 0)

    def start_list(a, src, dst):
        def one(s, c):
            p = list_peer(s)
            pltpu.make_async_remote_copy(
                src_ref=src.at[p], dst_ref=dst.at[me], send_sem=ar_ssem.at[a, 1], recv_sem=ar_rsem.at[a, 1],
                device_id={"list": p}, device_id_type=MESH).start()
            return c

        lax.fori_loop(1, NL, one, 0)

    def share_list(a, buf):
        def one(s, c):
            pltpu.make_async_remote_copy(
                src_ref=buf.at[me], dst_ref=buf.at[me], send_sem=ar_ssem.at[a, 2], recv_sem=ar_rsem.at[a, 2],
                device_id={"list": list_peer(s)}, device_id_type=MESH).start()
            return c

        lax.fori_loop(1, NL, one, 0)

    def share_dp(a, buf):
        def one(s, c):
            pltpu.make_async_remote_copy(
                src_ref=buf.at[dp], dst_ref=buf.at[dp], send_sem=ar_ssem.at[a, 3], recv_sem=ar_rsem.at[a, 3],
                device_id={"dp": dp_peer(s)}, device_id_type=MESH).start()
            return c

        lax.fori_loop(1, ND, one, 0)

    recv_sums, ls, lr, ag, ad = (dr0, dr1, dr2), (ls0, ls1, ls2), (lr0, lr1, lr2), (as0, as1, as2), (ad0, ad1, ad2)

    def sums_1(g):
        start_dp(g, send_sums[g], recv_sums[g])

    def sums_2(g):
        src, dst, width = send_sums[g], recv_sums[g], len(GROUPS[g])
        drain(dst.at[pl.ds(0, ND - 1)], ar_rsem.at[g, 0])
        dst[dp] = src[dp]
        total = dst[0]
        for q in range(1, ND):
            total = total + dst[q]
        for u in range(width):
            for p in range(NL):
                ls[g][p, u:u + 1, :] = total[u * 24 + p:u * 24 + p + 1]
                at = u * 24 + 16 + p // 8
                ls[g][p, width + u:width + u + 1, :] = total[at:at + 1]
        start_list(g, ls[g], lr[g])

    def sums_3(g):
        width = len(GROUPS[g])
        drain(lr[g].at[pl.ds(0, NL - 1)], ar_rsem.at[g, 1])
        lr[g][me] = ls[g][me]
        total = lr[g][0]
        for p in range(1, NL):
            total = total + lr[g][p]
        for u in range(width):
            m = GROUPS[g][u] * MC + dp * 2 + me // 8
            old = books[m, pl.ds(lax.rem(me, 8), 1), :]
            ag[g][me, u:u + 1, :] = (total[u:u + 1] + old) / (total[width + u:width + u + 1] + 1.0)
        share_list(g, ag[g])

    def sums_4(g):
        drain(ag[g].at[pl.ds(0, NL - 1)], ar_rsem.at[g, 2])
        for u in range(len(GROUPS[g])):
            for p in range(NL):
                ad[g][dp, u, p:p + 1, :] = ag[g][p, u:u + 1, :]
        share_dp(g, ad[g])

    def sums_5(g):
        drain(ad[g].at[pl.ds(0, ND - 1)], ar_rsem.at[g, 3])

    gs_, gr_, gl_, gm_, gt_, gd_ = (gsa, gsb), (gra, grb), (gla, glb), (gma, gmb), (gta, gtb), (gda, gdb)

    def gram_1(k):
        start_dp(3 + k, gs_[k], gr_[k])

    def gram_2(k):
        drain(gr_[k].at[pl.ds(0, ND - 1)], ar_rsem.at[3 + k, 0])
        blocks = gs_[k].shape[1]

        def one(b, c):
            total = gs_[k][dp, b].astype(F32)
            for s in range(1, ND):
                total = total + gr_[k][dp_peer(s), b].astype(F32)
            gl_[k][b] = total.astype(BF)
            return c

        lax.fori_loop(0, blocks, one, 0)
        for b in range(blocks, NL):
            gl_[k][b] = jnp.zeros((16, CW), BF)
        start_list(3 + k, gl_[k], gm_[k])

    def gram_3(k):
        drain(gm_[k].at[pl.ds(0, NL - 1)], ar_rsem.at[3 + k, 1])
        total = gl_[k][me].astype(F32)
        for s in range(1, NL):
            total = total + gm_[k][list_peer(s)].astype(F32)
        gt_[k][me] = total.astype(BF)
        share_list(3 + k, gt_[k])

    def gram_4(k):
        drain(gt_[k].at[pl.ds(0, NL - 1)], ar_rsem.at[3 + k, 2])
        gd_[k][dp] = gt_[k][...]
        share_dp(3 + k, gd_[k])

    def gram_5(k):
        drain(gd_[k].at[pl.ds(0, ND - 1)], ar_rsem.at[3 + k, 3])

    def rest_out(j):
        return pltpu.make_async_copy(rest.at[j], rest_hbm.at[j], out_sem.at[0])

    def chunk(g, u, j):
        drain(rbuf.at[j, pl.ds(0, NL - 1)], x_rsem.at[j])
        residual_chunk(j)
        hist_chunk(g, u, j)

    def group(g):
        first = GROUPS[g][0]

        def one(u, c):
            chunk(g, u, first + u)
            gram_chunk(gsa, first + u, block_of(first + u, 0))
            return c

        lax.fori_loop(0, len(GROUPS[g]), one, 0)

    group(0)
    sums_1(0)
    group(1)
    sums_1(1)
    gram_1(0)
    sums_2(0)
    chunk(2, 0, NC - 1)
    sums_1(2)
    sums_2(1)
    gram_2(0)
    sums_3(0)
    gram_chunk(gsb, NC - 1, 0)
    gram_1(1)
    sums_2(2)
    sums_3(1)
    gram_3(0)
    sums_4(0)
    gram_2(1)
    sums_3(2)
    sums_4(1)
    gram_4(0)
    gram_3(1)
    sums_4(2)
    gram_4(1)
    for g in range(3):
        sums_5(g)
    for k in range(2):
        gram_5(k)
    outs = [pltpu.make_async_copy(s, d, out_sem.at[i]) for i, (s, d) in enumerate(
        ((rest, rest_hbm), (ad0, nb0_hbm), (ad1, nb1_hbm), (ad2, nb2_hbm), (gda, ga_hbm), (gdb, gb_hbm)))]
    for o in outs:
        o.start()
    for j in range(NC):
        drain(sbuf.at[j, pl.ds(0, NL - 1)], x_ssem)
    for g in range(3):
        drain(send_sums[g].at[pl.ds(0, ND - 1)], ar_ssem.at[g, 0])
        drain(ls[g].at[pl.ds(0, NL - 1)], ar_ssem.at[g, 1])
        drain(ag[g].at[pl.ds(0, NL - 1)], ar_ssem.at[g, 2])
        drain(ad[g].at[pl.ds(0, ND - 1)], ar_ssem.at[g, 3])
    for k in range(2):
        drain(gs_[k].at[pl.ds(0, ND - 1)], ar_ssem.at[3 + k, 0])
        drain(gl_[k].at[pl.ds(0, NL - 1)], ar_ssem.at[3 + k, 1])
        drain(gt_[k].at[pl.ds(0, NL - 1)], ar_ssem.at[3 + k, 2])
        drain(gd_[k].at[pl.ds(0, ND - 1)], ar_ssem.at[3 + k, 3])
    for o in outs:
        o.wait()


def refine(ids, fill, vectors, codes, centroids, codebooks):
    anyspace = pl.BlockSpec(memory_space=pl.ANY)
    V = pltpu.VMEM
    widths = [len(g) for g in GROUPS]
    blocks = (15, 6)
    dma = pltpu.SemaphoreType.DMA
    out_shape = (
        [jax.ShapeDtypeStruct((NC, CW, SLOTS), BF)]
        + [jax.ShapeDtypeStruct((ND, w, NL, 256), F32) for w in widths]
        + [jax.ShapeDtypeStruct((ND, NL, 16, CW), BF) for _ in blocks]
    )
    scratch = (
        [
            V((NL, 1, CAP), jnp.int32), pltpu.SMEM((NL, 1, CAP), jnp.int32),
            V((4096, 8, 128), F32), V((2, 256, 768), BF), V((CAP, 8, 128), F32),
            V((NC, NL, CAP, CW), BF), V((NC, NL, CAP, CW), BF),
            V((SLOTS, 768), BF), V((NC, MC, SLOTS), jnp.int32), V((96, 8, 256), F32),
            V((NC, SLOTS, CW), BF), V((NC, CW, SLOTS), BF), V((16, SLOTS), BF), V((4, 144, 256), F32),
        ]
        + [V((ND, sum_rows(g), 256), F32) for g in range(3)] * 2
        + [V((NL, 2 * w, 256), F32) for w in widths] * 2
        + [V((NL, w, 256), F32) for w in widths]
        + [V((ND, w, NL, 256), F32) for w in widths]
        + [V((ND, b, 16, CW), BF) for b in blocks] * 2
        + [V((NL, 16, CW), BF) for _ in blocks] * 3
        + [V((ND, NL, 16, CW), BF) for _ in blocks]
        + [dma((3,)), dma((2,)), dma((6,)), dma, dma, dma, dma, dma((NC,)), dma((5, 4)), dma((5, 4))]
    )
    return pl.pallas_call(
        refine_kernel,
        out_shape=out_shape,
        in_specs=[pl.BlockSpec(memory_space=pltpu.VMEM), pl.BlockSpec(memory_space=pltpu.SMEM)] + [anyspace] * 4,
        out_specs=[anyspace] * 6,
        scratch_shapes=scratch,
        compiler_params=pltpu.CompilerParams(
            collective_id=0, has_side_effects=True, vmem_limit_bytes=60 << 20),
    )(ids, fill, vectors, codes, centroids, codebooks)


def error_kernel(fill_ref, rest_ref, codes_ref, nb0, nb1, nb2, ga, gb, err_ref, books_ref, gram_ref):
    step = pl.program_id(0)
    nb = (nb0, nb1, nb2)

    @pl.when(step == 0)
    def _():
        for g in range(3):
            for u, j in enumerate(GROUPS[g]):
                for q in range(ND):
                    for m2 in range(2):
                        books_ref[j * MC + q * 2 + m2] = nb[g][q, u, m2 * 8:m2 * 8 + 8, :]

    @pl.when(step == 1)
    def _():
        for j in range(NC):
            for i in range(j + 1):
                src, b = (ga, block_of(j, i)) if j < NC - 1 else (gb, i)
                block = jnp.concatenate([src[q, b].astype(F32) for q in range(ND)], 0)
                gram_ref[j * CW:(j + 1) * CW, i * CW:(i + 1) * CW] = block
                if i < j:
                    gram_ref[i * CW:(i + 1) * CW, j * CW:(j + 1) * CW] = block.T

    lane = lax.broadcasted_iota(jnp.int32, (8, 128), 1)
    used = lane < fill_ref[0, step]
    for g in range(3):
        for u, j in enumerate(GROUPS[g]):
            parts = []
            for m in range(MC):
                code = jnp.broadcast_to(codes_ref[j, m:m + 1, :], (8, 128))
                at = code & 127
                t = nb[g][m // 2, u, (m % 2) * 8:(m % 2) * 8 + 8, :]
                lo = jnp.take_along_axis(t[:, :128], at, axis=1, mode="promise_in_bounds")
                hi = jnp.take_along_axis(t[:, 128:], at, axis=1, mode="promise_in_bounds")
                parts.append(jnp.where(code < 128, lo, hi))
            r = rest_ref[j].astype(F32)
            e = r - jnp.concatenate(parts, 0)
            e = jnp.where(jnp.concatenate([used] * MC, 0), e, 0.0)
            err_ref[:, j * CW:(j + 1) * CW] = e.astype(BF).T


def local(vectors, list_ids, codes, fill_counts, centroids, codebooks):
    codes_t = codes.T.reshape(NC, MC, SLOTS)
    rest, nb0, nb1, nb2, ga, gb = refine(
        list_ids.reshape(NL, 1, CAP), fill_counts, vectors, codes_t, centroids, codebooks)
    whole = pl.BlockSpec(memory_space=pltpu.VMEM)
    err, books, gram = pl.pallas_call(
        error_kernel,
        grid=(NL,),
        out_shape=[
            jax.ShapeDtypeStruct((SLOTS, 768), BF),
            jax.ShapeDtypeStruct((96, 8, 256), F32),
            jax.ShapeDtypeStruct((768, 768), F32),
        ],
        in_specs=[
            pl.BlockSpec(memory_space=pltpu.SMEM),
            pl.BlockSpec((NC, CW, CAP), lambda i: (0, 0, i)),
            pl.BlockSpec((NC, MC, CAP), lambda i: (0, 0, i)),
        ] + [whole] * 5,
        out_specs=[
            pl.BlockSpec((CAP, 768), lambda i: (i, 0)),
            whole,
            whole,
        ],
        compiler_params=pltpu.CompilerParams(vmem_limit_bytes=40 << 20),
    )(fill_counts, rest, codes_t, nb0, nb1, nb2, ga, gb)
    return err, books, gram


def solution(mesh):
    in_specs = (
        P(("dp", "list"), None),
        P(("dp", "list")),
        P(("dp", "list"), None),
        P(("dp", "list"), None),
        P("list", None),
        P(),
    )
    out_specs = (P(("dp", "list"), None), P(), P())
    return jax.shard_map(local, mesh=mesh, in_specs=in_specs, out_specs=out_specs, check_vma=False)
```

time: 519 us -> 128 us (0.25)
  waiting for transfers between devices: 214 us -> 0 us
  matrix products: 144 us -> 0 us
  Pallas kernels: 0 us -> 120 us
  other arithmetic: 75.1 us -> 0 us
  local copies, waits for them, and re-layouts: 44.4 us -> 6.82 us
  blocking collectives: 14.9 us -> 0 us
  between operations: 14.1 us -> 0.69 us
  starting transfers between devices: 10.3 us -> 0 us
    psum x1 -> x0, waiting for transfers between devices: 159 us -> none  [local(): lax.psum((gram_part, sums, counts), ('dp', 'list'))]
    dot_general x17 -> x0, matrix products: 144 us -> none  [the longest x8 105 us: reconstruct(): jnp.einsum('rmk,mdk->rmd', onehot, new_books, precision=lax.Precision.HIG...]
    pallas_call x0 -> x2, Pallas kernels: none -> 120 us  [the longest x1 105 us: refine(): pl.pallas_call(refine_kernel, out_shape=out_shape, in_specs=[pl.BlockSpec...]
    reduce_sum x8 -> x0, other arithmetic: 65.4 us -> none  [accumulate(): counts = counts + jnp.sum(onehot.astype(jnp.float32), axis=0)]
    all_to_all x2 -> x0, waiting for transfers between devices: 55.6 us -> none  [the longest x1 32.4 us: local(): lax.all_to_all(diff, 'list', split_axis=0, concat_axis=0, tiled=True)]
    all_to_all x1 -> x0, blocking collectives: 14.9 us -> none  [local(): lax.all_to_all(id_blocks, 'list', split_axis=0, concat_axis=0, tiled=True)]
    eq x16 -> x0, local copies, waits for them, and re-layouts: 14.6 us -> none  [the longest x8 7.34 us: reconstruct(): onehot = (code_part[:, :, None] == kinds).astype(jnp.float32)]
    gather x1 -> x0, local copies, waits for them, and re-layouts: 13.7 us -> none  [local(): rows = jnp.take(centroids, wanted, axis=0)]
  transfers between devices with their start and end apart: 3 -> 0, of which waited for: 3 -> 0; matrix products, arithmetic and copies ran while one was open for 3% -> 0% of each run, Pallas kernels for 0% -> 0%
where the time goes in v1:
time: 128 us
  Pallas kernels  120 us (94%)
  local copies, waits for them, and re-layouts  6.82 us (5%)
    pallas_call x1, Pallas kernels, refine(): pl.pallas_call(refine_kernel, out_shape=out_shape, in_specs=[pl.BlockSpec...  105 us
    pallas_call x1, Pallas kernels, local(): pl.pallas_call(error_kernel, grid=(NL,), out_shape=[jax.ShapeDtypeStruct(...  15.5 us
    unnamed x16, local copies, waits for them, and re-layouts  6.82 us

profile of v1, /device:TPU:1, one launch (start us, length us, event | category | flops | bytes accessed | tf_op | source)
XLA Modules:
  0.0 127.9 jit_solution(3575184309783645916)
XLA Ops:
  0.6 0.0 copy-start.1
  0.6 0.0 copy-start.7
  0.7 104.8 %shard_map.85 = (bf16[6,128,2048]{2,1,0:T(8,128)(2,1)}, f32[8,3,16,256]{3,2,1,0:T(8,128)}, f32[8,2,16,256]{3,2,1,0:T(8,128)}, f32[8,1,16,256]{3,2,1,0:T(8,128)},...) custom-call(s32[16,1,128]{2,1,0:T(1,128)} %bitcast.6, s32[1,16]{1,0:T(1,128)} %fill_ref.3, ...), custom_call_target="tpu_custom_call" | custom-call | tf_op jit(solution)/shard_map/pallas_call | solution.py:488
  105.5 0.0 copy-done.1
  105.5 0.0 copy-done.7
  105.5 0.0 copy-start
  105.5 1.9 %copy-done = bf16[6,128,2048]{2,1,0:T(8,128)(2,1)S(1)} copy-done((bf16[6,128,2048]{2,1,0:T(8,128)(2,1)S(1)}, bf16[6,128,2048]{2,1,0:T(8,128)(2,1)}, u32[]{:S(2)}) %copy-start) | copy-done | bytes 3145752
  107.4 0.0 copy-start.2
  107.4 1.0 copy-done.2
  108.5 0.0 copy-start.3
  108.5 1.0 copy-done.3
  109.5 0.0 copy-start.4
  109.5 1.0 copy-done.4
  110.5 0.0 copy-start.5
  110.5 0.9 copy-done.5
  111.4 0.0 copy-start.6
  111.5 0.9 copy-done.6
  112.4 15.5 %shard_map.86 = (bf16[2048,768]{1,0:T(8,128)(2,1)}, f32[96,8,256]{2,1,0:T(8,128)}, f32[768,768]{1,0:T(8,128)}) custom-call(s32[1,16]{1,0:T(1,128)S(1)} %copy-done.7, bf16[6,128,2048]{2,1,0:T(8,128)(2,1)S(1)} %copy-done, s32[6,16,2048]{2,1,0:T(8,128)S(1)} %bitcast.5, f32[8,3,16,256]{3,2,1,0:T(8,128)S(1)} %copy-done.4, f32[8,2,16,256]{3,2,1,0:T(8,128)S(1)} %copy-done.5, ...), custom_call_target="tpu_custom_call" | custom-call | tf_op jit(solution)/shard_map/pallas_call | solution.py:544
Async XLA Ops:
  0.6 104.9 %copy-start.1 = (s32[2048,96]{0,1:T(8,128)S(1)}, s32[2048,96]{0,1:T(8,128)}, u32[]{:S(2)}) copy-start(s32[2048,96]{0,1:T(8,128)} %param.8) | copy-start | bytes 2359300
  0.6 104.9 %copy-start.7 = (s32[1,16]{1,0:T(1,128)S(1)}, s32[1,16]{1,0:T(1,128)}, u32[]{:S(2)}) copy-start(s32[1,16]{1,0:T(1,128)} %fill_ref.3) | copy-start | bytes 196
  105.5 1.9 %copy-start = (bf16[6,128,2048]{2,1,0:T(8,128)(2,1)S(1)}, bf16[6,128,2048]{2,1,0:T(8,128)(2,1)}, u32[]{:S(2)}) copy-start(bf16[6,128,2048]{2,1,0:T(8,128)(2,1)} %get-tuple-element.9.rest_ref) | copy-start | bytes 9437188
  107.4 1.0 copy-start.2
  108.5 1.0 copy-start.3
  109.5 1.0 copy-start.4
  110.5 0.9 copy-start.5
  111.4 0.9 copy-start.6

commit v2 on v1

--- a/solution.py
+++ b/solution.py
@@ -16,8 +16,9 @@
 NC = 6
 CW = 128
 MC = 16
-GROUPS = ((0, 1, 2), (3, 4), (5,))
-GSTEP = 512
+GROUPS = ((0, 1), (2, 3, 4), (5,))
+GSTEP = 1024
+AHEAD = 2
 
 
 def sum_rows(g):
@@ -34,8 +35,8 @@
 
 def refine_kernel(
     ids_ref, fill_ref, vec_hbm, codes_hbm, cent_hbm, books_hbm,
-    rest_hbm, nb0_hbm, nb1_hbm, nb2_hbm, ga_hbm, gb_hbm,
-    ids_in, ids_s, table, cbuf, gbuf, sbuf, rbuf, vec, codes, books, res, rest, live, acc,
+    err_hbm, nb_hbm, gram_hbm,
+    ids_in, ids_s, table, cbuf, gbuf, sbuf, rbuf, vec, codes, books, res, rest, live, acc, err, gram,
     ds0, ds1, ds2, dr0, dr1, dr2, ls0, ls1, ls2, lr0, lr1, lr2,
     as0, as1, as2, ad0, ad1, ad2,
     gsa, gsb, gra, grb, gla, glb, gma, gmb, gta, gtb, gda, gdb,
@@ -52,19 +53,21 @@
     def dp_peer(s):
         return lax.rem(dp + s, ND)
 
-    cent_rows = cbuf.shape[1]
-    n_cent = cent_hbm.shape[0] // cent_rows
+    n_cent = cent_sem.shape[0]
+    cent_rows = cbuf.shape[0] // n_cent
 
     def cent_copy(b):
-        slot = lax.rem(b, 2)
-        return pltpu.make_async_copy(
-            cent_hbm.at[pl.ds(b * cent_rows, cent_rows)], cbuf.at[slot], cent_sem.at[slot])
+        rows = pl.ds(pl.multiple_of(b * cent_rows, cent_rows), cent_rows)
+        return pltpu.make_async_copy(cent_hbm.at[rows], cbuf.at[rows], cent_sem.at[b])
 
     codes_load = pltpu.make_async_copy(codes_hbm, codes, load_sem.at[0])
     books_load = pltpu.make_async_copy(books_hbm, books, load_sem.at[1])
     vec_load = pltpu.make_async_copy(vec_hbm, vec, load_sem.at[2])
-    cent_copy(0).start()
-    cent_copy(1).start()
+    for b in range(n_cent):
+        cent_copy(b).start()
+    vec_load.start()
+    codes_load.start()
+    books_load.start()
 
     barrier = pltpu.get_barrier_semaphore()
 
@@ -78,7 +81,6 @@
 
     lax.fori_loop(1, NL, greet_list, 0)
     lax.fori_loop(1, ND, greet_dp, 0)
-    pl.semaphore_wait(barrier, NL + ND - 2)
 
     def send_ids(s, c):
         p = list_peer(s)
@@ -87,36 +89,31 @@
             device_id={"list": p}, device_id_type=MESH).start()
         return c
 
-    lax.fori_loop(1, NL, send_ids, 0)
-    vec_load.start()
-    codes_load.start()
-    books_load.start()
-    ids_in[me] = ids_ref[me]
 
     table_rows = table.reshape(4096 * 8, 128)
-    gathered_rows = gbuf.reshape(CAP * 8, 128)
+    gathered_rows = gbuf.reshape(32 * 8, 128)
 
     def build(b, c):
         cent_copy(b).wait()
-        slot = lax.rem(b, 2)
 
         def rows16(r, c):
+            row = pl.multiple_of(b * cent_rows + r * 16, 16)
             for j in range(NC):
-                v = cbuf[slot, pl.ds(pl.multiple_of(r * 16, 16), 16), j * CW:(j + 1) * CW].astype(F32)
-                base = (b * cent_rows + r * 16) * 8
-                table_rows[pl.ds(base + j, 8, stride=8), :] = v[:8]
-                table_rows[pl.ds(base + 64 + j, 8, stride=8), :] = v[8:]
-            return c
-
-        lax.fori_loop(0, cent_rows // 16, rows16, 0)
-
-        @pl.when(b + 2 < n_cent)
-        def _():
-            cent_copy(b + 2).start()
-
-        return c
+                v = cbuf[pl.ds(row, 16), j * CW:(j + 1) * CW].astype(F32)
+                table_rows[pl.ds(row * 8 + j, 8, stride=8), :] = v[:8]
+                table_rows[pl.ds(row * 8 + 64 + j, 8, stride=8), :] = v[8:]
+            return c
+
+        return lax.fori_loop(0, cent_rows // 16, rows16, c, unroll=4)
 
     lax.fori_loop(0, n_cent, build, 0)
+    pl.semaphore_wait(barrier, NL + ND - 2)
+    lax.fori_loop(1, NL, send_ids, 0)
+    ids_in[me] = ids_ref[me]
+
+    lane = lax.broadcasted_iota(jnp.int32, (16, CAP), 1)
+    for p in range(NL):
+        live[:, p * CAP:(p + 1) * CAP] = (lane < fill_ref[0, p]).astype(F32).astype(BF)
 
     drain(ids_in.at[pl.ds(0, NL - 1)], ids_rsem)
     drain(ids_in.at[pl.ds(0, NL - 1)], ids_ssem)
@@ -129,56 +126,39 @@
             src_ref=sbuf.at[j, p], dst_ref=rbuf.at[j, me], send_sem=x_ssem, recv_sem=x_rsem.at[j],
             device_id={"list": p}, device_id_type=MESH)
 
-    def gather(p):
+    def gather(p, dst):
         def rows(r, c):
-            for k in range(16):
-                at = r * 16 + k
-                row = ids_s[p, 0, at]
-                gbuf[at] = table[row]
-            return c
-
-        lax.fori_loop(0, CAP // 16, rows, 0)
-
-        def pack(r, c):
-            for j in range(NC):
-                lo = gathered_rows[pl.ds(r * 128 + j, 8, stride=8), :]
-                hi = gathered_rows[pl.ds(r * 128 + 64 + j, 8, stride=8), :]
-                sbuf[j, p, pl.ds(pl.multiple_of(r * 16, 16), 16), :] = jnp.concatenate([lo, hi], 0).astype(BF)
-            return c
-
-        lax.fori_loop(0, CAP // 16, pack, 0)
+            for half in range(2):
+                for k in range(16):
+                    row = ids_s[p, 0, r * 32 + half * 16 + k]
+                    gbuf[half * 16 + k] = table[row]
+            for half in range(2):
+                at = pl.ds(pl.multiple_of(r * 32 + half * 16, 16), 16)
+                for j in range(NC):
+                    lo = gathered_rows[pl.ds(half * 128 + j, 8, stride=8), :]
+                    hi = gathered_rows[pl.ds(half * 128 + 64 + j, 8, stride=8), :]
+                    dst[j, p, at, :] = jnp.concatenate([lo, hi], 0).astype(BF)
+            return c
+
+        lax.fori_loop(0, CAP // 32, rows, 0)
 
     def gather_send(s, c):
         p = list_peer(s)
-        gather(p)
-        x_copy(0, p).start()
+        gather(p, sbuf)
+        for j in range(AHEAD):
+            x_copy(j, p).start()
         return c
 
     lax.fori_loop(1, NL, gather_send, 0)
 
-    def send_chunk(j, c):
+    def send_chunk(j):
         def one(s, c):
             x_copy(j, list_peer(s)).start()
             return c
 
-        return lax.fori_loop(1, NL, one, c)
-
-    lax.fori_loop(1, NC, send_chunk, 0)
-    gather(me)
-
-    def own(j, c):
-        def rows(r, c):
-            at = pl.ds(pl.multiple_of(r * 16, 16), 16)
-            rbuf[j, me, at, :] = sbuf[j, me, at, :]
-            return c
-
-        return lax.fori_loop(0, CAP // 16, rows, c)
-
-    lax.fori_loop(0, NC, own, 0)
-
-    lane = lax.broadcasted_iota(jnp.int32, (16, CAP), 1)
-    for p in range(NL):
-        live[:, p * CAP:(p + 1) * CAP] = (lane < fill_ref[0, p]).astype(F32).astype(BF)
+        lax.fori_loop(1, NL, one, 0)
+
+    gather(me, rbuf)
 
     vec_load.wait()
     codes_load.wait()
@@ -202,7 +182,7 @@
             rest[j, :, pl.ds(pl.multiple_of(p * CAP, CAP), CAP)] = d.T
             return c
 
-        lax.fori_loop(0, NL, one, 0)
+        lax.fori_loop(0, NL, one, 0, unroll=4)
 
     def hist_chunk(g, u, j):
         acc[...] = jnp.zeros_like(acc)
@@ -265,14 +245,14 @@
                     buf[q, pl.ds(base + 16, 8), out] = jnp.where(row8 == 0, cnt[0], cnt[1])
 
     def gram_chunk(buf, j, first):
-        def one(i, c):
+        for i in range(0, j + 1, 2):
+            wide = min(2, j + 1 - i)
+            right = jnp.concatenate([res[i + k] for k in range(wide)], 1)
             block = lax.dot_general(
-                rest[j], res[i], (((1,), (0,)), ((), ())), preferred_element_type=F32) * (1.0 / (SLOTS * NL * ND))
-            for q in range(ND):
-                buf[q, first + i] = block[q * 16:q * 16 + 16].astype(BF)
-            return c
-
-        lax.fori_loop(0, j + 1, one, 0)
+                rest[j], right, (((1,), (0,)), ((), ())), preferred_element_type=F32) * (1.0 / (SLOTS * NL * ND))
+            for k in range(wide):
+                for q in range(ND):
+                    buf[q, first + i + k] = block[q * 16:q * 16 + 16, k * CW:(k + 1) * CW].astype(BF)
 
     def start_dp(a, src, dst):
         def one(s, c):
@@ -385,61 +365,116 @@
 
     def gram_4(k):
         drain(gt_[k].at[pl.ds(0, NL - 1)], ar_rsem.at[3 + k, 2])
-        gd_[k][dp] = gt_[k][...]
+        gd_[k][dp] = gt_[k][:gd_[k].shape[1]]
         share_dp(3 + k, gd_[k])
 
     def gram_5(k):
         drain(gd_[k].at[pl.ds(0, ND - 1)], ar_rsem.at[3 + k, 3])
 
-    def rest_out(j):
-        return pltpu.make_async_copy(rest.at[j], rest_hbm.at[j], out_sem.at[0])
+    def err_out(j):
+        return pltpu.make_async_copy(
+            err.at[j], err_hbm.at[:, pl.ds(pl.multiple_of(j * CW, CW), CW)], out_sem.at[0])
+
+    def error_chunk(g, u, j):
+        def one(p, c):
+            at = pl.ds(pl.multiple_of(p * CAP, CAP), CAP)
+            used = lane128 < fill_ref[0, p]
+            parts = []
+            for m in range(MC):
+                code = jnp.broadcast_to(codes[j, m:m + 1, at], (8, 128))
+                k = code & 127
+                t = ad[g][m // 2, u, (m % 2) * 8:(m % 2) * 8 + 8, :]
+                lo = jnp.take_along_axis(t[:, :128], k, axis=1, mode="promise_in_bounds")
+                hi = jnp.take_along_axis(t[:, 128:], k, axis=1, mode="promise_in_bounds")
+                r = rest[j, m * 8:m * 8 + 8, at].astype(F32)
+                parts.append(jnp.where(used, r - jnp.where(code < 128, lo, hi), 0.0))
+            err[j, at, :] = jnp.concatenate(parts, 0).astype(BF).T
+            return c
+
+        lax.fori_loop(0, NL, one, 0, unroll=4)
+        err_out(j).start()
+
+    def book_outs(g):
+        return [pltpu.make_async_copy(ad[g].at[:, u], nb_hbm.at[j], out_sem.at[1]) for u, j in enumerate(GROUPS[g])]
+
+    def gram_rows(buf, j, first):
+        def one(i, c):
+            block = jnp.concatenate([buf[q, first + i].astype(F32) for q in range(ND)], 0)
+            jr = pl.ds(pl.multiple_of(j * CW, CW), CW)
+            ir = pl.ds(pl.multiple_of(i * CW, CW), CW)
+            gram[ir, jr] = block.T
+            gram[jr, ir] = block
+            return c
+
+        lax.fori_loop(0, j + 1, one, 0)
 
     def chunk(g, u, j):
         drain(rbuf.at[j, pl.ds(0, NL - 1)], x_rsem.at[j])
+        if isinstance(j, int):
+            if j + AHEAD < NC:
+                send_chunk(j + AHEAD)
+        else:
+            send_chunk(j + AHEAD)
         residual_chunk(j)
         hist_chunk(g, u, j)
 
-    def group(g):
-        first = GROUPS[g][0]
-
-        def one(u, c):
-            chunk(g, u, first + u)
-            gram_chunk(gsa, first + u, block_of(first + u, 0))
-            return c
-
-        lax.fori_loop(0, len(GROUPS[g]), one, 0)
-
-    group(0)
+    def gram_early(j):
+        gram_chunk(gsa, j, block_of(j, 0))
+
+    chunk(0, 0, 0)
+    gram_early(0)
+    chunk(0, 1, 1)
     sums_1(0)
-    group(1)
+    gram_early(1)
+    chunk(1, 0, 2)
+    gram_early(2)
+    sums_2(0)
+    chunk(1, 1, 3)
+    gram_early(3)
+    chunk(1, 2, 4)
     sums_1(1)
+    gram_early(4)
     gram_1(0)
-    sums_2(0)
-    chunk(2, 0, NC - 1)
+    sums_3(0)
+    chunk(2, 0, 5)
     sums_1(2)
     sums_2(1)
     gram_2(0)
-    sums_3(0)
     gram_chunk(gsb, NC - 1, 0)
     gram_1(1)
+    sums_4(0)
     sums_2(2)
+    gram_2(1)
     sums_3(1)
     gram_3(0)
-    sums_4(0)
-    gram_2(1)
+    sums_5(0)
+    error_chunk(0, 0, 0)
     sums_3(2)
+    gram_3(1)
     sums_4(1)
     gram_4(0)
-    gram_3(1)
+    error_chunk(0, 1, 1)
     sums_4(2)
     gram_4(1)
-    for g in range(3):
-        sums_5(g)
-    for k in range(2):
-        gram_5(k)
-    outs = [pltpu.make_async_copy(s, d, out_sem.at[i]) for i, (s, d) in enumerate(
-        ((rest, rest_hbm), (ad0, nb0_hbm), (ad1, nb1_hbm), (ad2, nb2_hbm), (gda, ga_hbm), (gdb, gb_hbm)))]
-    for o in outs:
+    sums_5(1)
+    error_chunk(1, 0, 2)
+    error_chunk(1, 1, 3)
+    sums_5(2)
+    error_chunk(2, 0, 5)
+    error_chunk(1, 2, 4)
+    gram_5(0)
+
+    def early_rows(j, c):
+        gram_rows(gda, j, block_of(j, 0))
+        return c
+
+    lax.fori_loop(0, NC - 1, early_rows, 0)
+    gram_5(1)
+    gram_rows(gdb, NC - 1, 0)
+    gram_out = pltpu.make_async_copy(gram, gram_hbm, out_sem.at[2])
+    gram_out.start()
+    books_out = [o for g in range(3) for o in book_outs(g)]
+    for o in books_out:
         o.start()
     for j in range(NC):
         drain(sbuf.at[j, pl.ds(0, NL - 1)], x_ssem)
@@ -453,8 +488,11 @@
         drain(gl_[k].at[pl.ds(0, NL - 1)], ar_ssem.at[3 + k, 1])
         drain(gt_[k].at[pl.ds(0, NL - 1)], ar_ssem.at[3 + k, 2])
         drain(gd_[k].at[pl.ds(0, ND - 1)], ar_ssem.at[3 + k, 3])
-    for o in outs:
+    for j in range(NC):
+        err_out(j).wait()
+    for o in books_out:
         o.wait()
+    gram_out.wait()
 
 
 def refine(ids, fill, vectors, codes, centroids, codebooks):
@@ -463,18 +501,19 @@
     widths = [len(g) for g in GROUPS]
     blocks = (15, 6)
     dma = pltpu.SemaphoreType.DMA
-    out_shape = (
-        [jax.ShapeDtypeStruct((NC, CW, SLOTS), BF)]
-        + [jax.ShapeDtypeStruct((ND, w, NL, 256), F32) for w in widths]
-        + [jax.ShapeDtypeStruct((ND, NL, 16, CW), BF) for _ in blocks]
-    )
+    out_shape = [
+        jax.ShapeDtypeStruct((SLOTS, 768), BF),
+        jax.ShapeDtypeStruct((NC, ND, 16, 256), F32),
+        jax.ShapeDtypeStruct((768, 768), F32),
+    ]
     scratch = (
         [
             V((NL, 1, CAP), jnp.int32), pltpu.SMEM((NL, 1, CAP), jnp.int32),
-            V((4096, 8, 128), F32), V((2, 256, 768), BF), V((CAP, 8, 128), F32),
+            V((4096, 8, 128), F32), V((4096, 768), BF), V((32, 8, 128), F32),
             V((NC, NL, CAP, CW), BF), V((NC, NL, CAP, CW), BF),
             V((SLOTS, 768), BF), V((NC, MC, SLOTS), jnp.int32), V((96, 8, 256), F32),
             V((NC, SLOTS, CW), BF), V((NC, CW, SLOTS), BF), V((16, SLOTS), BF), V((4, 144, 256), F32),
+            V((NC, SLOTS, CW), BF), V((768, 768), F32),
         ]
         + [V((ND, sum_rows(g), 256), F32) for g in range(3)] * 2
         + [V((NL, 2 * w, 256), F32) for w in widths] * 2
@@ -482,86 +521,25 @@
         + [V((ND, w, NL, 256), F32) for w in widths]
         + [V((ND, b, 16, CW), BF) for b in blocks] * 2
         + [V((NL, 16, CW), BF) for _ in blocks] * 3
-        + [V((ND, NL, 16, CW), BF) for _ in blocks]
-        + [dma((3,)), dma((2,)), dma((6,)), dma, dma, dma, dma, dma((NC,)), dma((5, 4)), dma((5, 4))]
+        + [V((ND, n, 16, CW), BF) for n in (NL, 6)]
+        + [dma((3,)), dma((8,)), dma((3,)), dma, dma, dma, dma, dma((NC,)), dma((5, 4)), dma((5, 4))]
     )
     return pl.pallas_call(
         refine_kernel,
         out_shape=out_shape,
         in_specs=[pl.BlockSpec(memory_space=pltpu.VMEM), pl.BlockSpec(memory_space=pltpu.SMEM)] + [anyspace] * 4,
-        out_specs=[anyspace] * 6,
+        out_specs=[anyspace] * 3,
         scratch_shapes=scratch,
         compiler_params=pltpu.CompilerParams(
             collective_id=0, has_side_effects=True, vmem_limit_bytes=60 << 20),
     )(ids, fill, vectors, codes, centroids, codebooks)
 
 
-def error_kernel(fill_ref, rest_ref, codes_ref, nb0, nb1, nb2, ga, gb, err_ref, books_ref, gram_ref):
-    step = pl.program_id(0)
-    nb = (nb0, nb1, nb2)
-
-    @pl.when(step == 0)
-    def _():
-        for g in range(3):
-            for u, j in enumerate(GROUPS[g]):
-                for q in range(ND):
-                    for m2 in range(2):
-                        books_ref[j * MC + q * 2 + m2] = nb[g][q, u, m2 * 8:m2 * 8 + 8, :]
-
-    @pl.when(step == 1)
-    def _():
-        for j in range(NC):
-            for i in range(j + 1):
-                src, b = (ga, block_of(j, i)) if j < NC - 1 else (gb, i)
-                block = jnp.concatenate([src[q, b].astype(F32) for q in range(ND)], 0)
-                gram_ref[j * CW:(j + 1) * CW, i * CW:(i + 1) * CW] = block
-                if i < j:
-                    gram_ref[i * CW:(i + 1) * CW, j * CW:(j + 1) * CW] = block.T
-
-    lane = lax.broadcasted_iota(jnp.int32, (8, 128), 1)
-    used = lane < fill_ref[0, step]
-    for g in range(3):
-        for u, j in enumerate(GROUPS[g]):
-            parts = []
-            for m in range(MC):
-                code = jnp.broadcast_to(codes_ref[j, m:m + 1, :], (8, 128))
-                at = code & 127
-                t = nb[g][m // 2, u, (m % 2) * 8:(m % 2) * 8 + 8, :]
-                lo = jnp.take_along_axis(t[:, :128], at, axis=1, mode="promise_in_bounds")
-                hi = jnp.take_along_axis(t[:, 128:], at, axis=1, mode="promise_in_bounds")
-                parts.append(jnp.where(code < 128, lo, hi))
-            r = rest_ref[j].astype(F32)
-            e = r - jnp.concatenate(parts, 0)
-            e = jnp.where(jnp.concatenate([used] * MC, 0), e, 0.0)
-            err_ref[:, j * CW:(j + 1) * CW] = e.astype(BF).T
-
-
 def local(vectors, list_ids, codes, fill_counts, centroids, codebooks):
     codes_t = codes.T.reshape(NC, MC, SLOTS)
-    rest, nb0, nb1, nb2, ga, gb = refine(
+    err, books, gram = refine(
         list_ids.reshape(NL, 1, CAP), fill_counts, vectors, codes_t, centroids, codebooks)
-    whole = pl.BlockSpec(memory_space=pltpu.VMEM)
-    err, books, gram = pl.pallas_call(
-        error_kernel,
-        grid=(NL,),
-        out_shape=[
-            jax.ShapeDtypeStruct((SLOTS, 768), BF),
-            jax.ShapeDtypeStruct((96, 8, 256), F32),
-            jax.ShapeDtypeStruct((768, 768), F32),
-        ],
-        in_specs=[
-            pl.BlockSpec(memory_space=pltpu.SMEM),
-            pl.BlockSpec((NC, CW, CAP), lambda i: (0, 0, i)),
-            pl.BlockSpec((NC, MC, CAP), lambda i: (0, 0, i)),
-        ] + [whole] * 5,
-        out_specs=[
-            pl.BlockSpec((CAP, 768), lambda i: (i, 0)),
-            whole,
-            whole,
-        ],
-        compiler_params=pltpu.CompilerParams(vmem_limit_bytes=40 << 20),
-    )(fill_counts, rest, codes_t, nb0, nb1, nb2, ga, gb)
-    return err, books, gram
+    return err, books.reshape(96, 8, 256), gram
 
 
 def solution(mesh):

time: 128 us -> 111 us (0.87)
  Pallas kernels: 120 us -> 104 us
    pallas_call x1 -> x0, Pallas kernels: 15.5 us -> none  [local(): pl.pallas_call(error_kernel, grid=(NL,), out_shape=[jax.ShapeDtypeStruct(...]
    unnamed x16 -> x7, local copies, waits for them, and re-layouts: 6.82 us -> 6.2 us
where the time goes in v2:
time: 111 us
  Pallas kernels  104 us (94%)
  local copies, waits for them, and re-layouts  6.2 us (6%)
    pallas_call x1, Pallas kernels, refine(): pl.pallas_call(refine_kernel, out_shape=out_shape, in_specs=[pl.BlockSpec...  104 us
    unnamed x7, local copies, waits for them, and re-layouts  6.2 us

profile of v2, /device:TPU:1, one launch (start us, length us, event | category | flops | bytes accessed | tf_op | source)
XLA Modules:
  0.0 110.8 jit_solution(6239378345800057853)
XLA Ops:
  0.6 104.0 %shard_map.85 = (bf16[2048,768]{1,0:T(8,128)(2,1)}, f32[6,8,16,256]{3,2,1,0:T(8,128)}, f32[768,768]{1,0:T(8,128)}) custom-call(s32[16,1,128]{2,1,0:T(1,128)} %bitcast.7, s32[1,16]{1,0:T(1,128)} %fill_ref.1, bf16[2048,768]{1,0:T(8,128)(2,1)} %vec_hbm.1, s32[6,16,2048]{2,1,0:T(8,128)} %bitcast.5, bf16[4096,768]{1,0:T(8,128)(2,1)} %cent_hbm.1, ...), custom_call_target="tpu_custom_call" | custom-call | tf_op jit(solution)/shard_map/pallas_call | solution.py:527
  104.6 0.0 copy-start.1
  104.6 0.0 copy-start
  104.6 3.9 %copy.12 = bf16[2048,768]{1,0:T(8,128)(2,1)} copy(bf16[2048,768]{1,0:T(8,128)(2,1)} %get-tuple-element.12) | data formatting | bytes 6291456
  108.6 0.0 copy-done.1
  108.6 0.9 copy.13
  109.4 0.0 copy-done
  109.4 1.4 %copy.14 = f32[768,768]{1,0:T(8,128)} copy(f32[768,768]{1,0:T(8,128)S(1)} %copy-done) | data formatting | bytes 4718592
Async XLA Ops:
  104.6 3.9 %copy-start.1 = (f32[6,8,16,256]{3,2,1,0:T(8,128)S(1)}, f32[6,8,16,256]{3,2,1,0:T(8,128)}, u32[]{:S(2)}) copy-start(f32[6,8,16,256]{3,2,1,0:T(8,128)} %get-tuple-element.7) | copy-start | bytes 2359300
  104.6 4.8 %copy-start = (f32[768,768]{1,0:T(8,128)S(1)}, f32[768,768]{1,0:T(8,128)}, u32[]{:S(2)}) copy-start(f32[768,768]{1,0:T(8,128)} %get-tuple-element.14) | copy-start | bytes 7077892

commit v3 on v2

--- a/solution.py
+++ b/solution.py
@@ -16,7 +16,7 @@
 NC = 6
 CW = 128
 MC = 16
-GROUPS = ((0, 1), (2, 3, 4), (5,))
+GROUPS = ((0, 1), (2, 3), (4, 5))
 GSTEP = 1024
 AHEAD = 2
 
@@ -35,8 +35,8 @@
 
 def refine_kernel(
     ids_ref, fill_ref, vec_hbm, codes_hbm, cent_hbm, books_hbm,
-    err_hbm, nb_hbm, gram_hbm,
-    ids_in, ids_s, table, cbuf, gbuf, sbuf, rbuf, vec, codes, books, res, rest, live, acc, err, gram,
+    err_hbm, nb_hbm, ga_hbm, gb_hbm,
+    ids_in, ids_s, table, cbuf, gbuf, sbuf, rbuf, vec, codes, books, res, rest, live, acc, err,
     ds0, ds1, ds2, dr0, dr1, dr2, ls0, ls1, ls2, lr0, lr1, lr2,
     as0, as1, as2, ad0, ad1, ad2,
     gsa, gsb, gra, grb, gla, glb, gma, gmb, gta, gtb, gda, gdb,
@@ -145,8 +145,7 @@
     def gather_send(s, c):
         p = list_peer(s)
         gather(p, sbuf)
-        for j in range(AHEAD):
-            x_copy(j, p).start()
+        x_copy(0, p).start()
         return c
 
     lax.fori_loop(1, NL, gather_send, 0)
@@ -158,6 +157,7 @@
 
         lax.fori_loop(1, NL, one, 0)
 
+    send_chunk(1)
     gather(me, rbuf)
 
     vec_load.wait()
@@ -360,16 +360,48 @@
         total = gl_[k][me].astype(F32)
         for s in range(1, NL):
             total = total + gm_[k][list_peer(s)].astype(F32)
-        gt_[k][me] = total.astype(BF)
-        share_list(3 + k, gt_[k])
+        mine = pl.ds(pl.multiple_of(dp * 16, 16), 16)
+        gt_[k][mine, :] = total.astype(BF)
+
+        def one(s, c):
+            pltpu.make_async_remote_copy(
+                src_ref=gt_[k].at[mine], dst_ref=gt_[k].at[mine], send_sem=ar_ssem.at[3 + k, 2],
+                recv_sem=ar_rsem.at[3 + k, 2], device_id={"dp": dp_peer(s)}, device_id_type=MESH).start()
+            return c
+
+        lax.fori_loop(1, ND, one, 0)
+
+    def with_block(k, yes, no=None):
+        owners = gd_[k].shape[0]
+        if owners == NL:
+            yes()
+        else:
+            pl.when(me < owners)(yes)
+            if no is not None:
+                pl.when(me >= owners)(no)
 
     def gram_4(k):
-        drain(gt_[k].at[pl.ds(0, NL - 1)], ar_rsem.at[3 + k, 2])
-        gd_[k][dp] = gt_[k][:gd_[k].shape[1]]
-        share_dp(3 + k, gd_[k])
+        drain(gt_[k].at[pl.ds(0, 112)], ar_rsem.at[3 + k, 2])
+
+        def send():
+            gd_[k][me] = gt_[k][...]
+
+            def one(s, c):
+                pltpu.make_async_remote_copy(
+                    src_ref=gt_[k], dst_ref=gd_[k].at[me], send_sem=ar_ssem.at[3 + k, 3],
+                    recv_sem=ar_rsem.at[3 + k, 3], device_id={"list": list_peer(s)}, device_id_type=MESH).start()
+                return c
+
+            lax.fori_loop(1, NL, one, 0)
+
+        with_block(k, send)
 
     def gram_5(k):
-        drain(gd_[k].at[pl.ds(0, ND - 1)], ar_rsem.at[3 + k, 3])
+        owners = gd_[k].shape[0]
+        with_block(
+            k,
+            lambda: drain(gd_[k].at[pl.ds(0, owners - 1)], ar_rsem.at[3 + k, 3]),
+            lambda: drain(gd_[k], ar_rsem.at[3 + k, 3]))
 
     def err_out(j):
         return pltpu.make_async_copy(
@@ -397,23 +429,11 @@
     def book_outs(g):
         return [pltpu.make_async_copy(ad[g].at[:, u], nb_hbm.at[j], out_sem.at[1]) for u, j in enumerate(GROUPS[g])]
 
-    def gram_rows(buf, j, first):
-        def one(i, c):
-            block = jnp.concatenate([buf[q, first + i].astype(F32) for q in range(ND)], 0)
-            jr = pl.ds(pl.multiple_of(j * CW, CW), CW)
-            ir = pl.ds(pl.multiple_of(i * CW, CW), CW)
-            gram[ir, jr] = block.T
-            gram[jr, ir] = block
-            return c
-
-        lax.fori_loop(0, j + 1, one, 0)
-
-    def chunk(g, u, j):
+    def chunk(g, u, j, arrived=None):
         drain(rbuf.at[j, pl.ds(0, NL - 1)], x_rsem.at[j])
-        if isinstance(j, int):
-            if j + AHEAD < NC:
-                send_chunk(j + AHEAD)
-        else:
+        if arrived is not None:
+            arrived(0)
+        if j + AHEAD < NC:
             send_chunk(j + AHEAD)
         residual_chunk(j)
         hist_chunk(g, u, j)
@@ -428,53 +448,41 @@
     gram_early(1)
     chunk(1, 0, 2)
     gram_early(2)
-    sums_2(0)
-    chunk(1, 1, 3)
+    chunk(1, 1, 3, sums_2)
+    sums_1(1)
     gram_early(3)
-    chunk(1, 2, 4)
-    sums_1(1)
+    chunk(2, 0, 4, sums_3)
     gram_early(4)
     gram_1(0)
-    sums_3(0)
-    chunk(2, 0, 5)
+    chunk(2, 1, 5, lambda g: (sums_4(0), sums_2(1)))
     sums_1(2)
-    sums_2(1)
-    gram_2(0)
     gram_chunk(gsb, NC - 1, 0)
     gram_1(1)
-    sums_4(0)
+    gram_2(0)
+    sums_3(1)
     sums_2(2)
     gram_2(1)
-    sums_3(1)
-    gram_3(0)
     sums_5(0)
     error_chunk(0, 0, 0)
+    sums_4(1)
     sums_3(2)
+    gram_3(0)
     gram_3(1)
-    sums_4(1)
-    gram_4(0)
     error_chunk(0, 1, 1)
     sums_4(2)
     gram_4(1)
+    gram_4(0)
     sums_5(1)
     error_chunk(1, 0, 2)
     error_chunk(1, 1, 3)
     sums_5(2)
-    error_chunk(2, 0, 5)
-    error_chunk(1, 2, 4)
+    error_chunk(2, 0, 4)
+    error_chunk(2, 1, 5)
+    gram_5(1)
     gram_5(0)
-
-    def early_rows(j, c):
-        gram_rows(gda, j, block_of(j, 0))
-        return c
-
-    lax.fori_loop(0, NC - 1, early_rows, 0)
-    gram_5(1)
-    gram_rows(gdb, NC - 1, 0)
-    gram_out = pltpu.make_async_copy(gram, gram_hbm, out_sem.at[2])
-    gram_out.start()
-    books_out = [o for g in range(3) for o in book_outs(g)]
-    for o in books_out:
+    outs = [o for g in range(3) for o in book_outs(g)]
+    outs += [pltpu.make_async_copy(gda, ga_hbm, out_sem.at[2]), pltpu.make_async_copy(gdb, gb_hbm, out_sem.at[2])]
+    for o in outs:
         o.start()
     for j in range(NC):
         drain(sbuf.at[j, pl.ds(0, NL - 1)], x_ssem)
@@ -486,13 +494,12 @@
     for k in range(2):
         drain(gs_[k].at[pl.ds(0, ND - 1)], ar_ssem.at[3 + k, 0])
         drain(gl_[k].at[pl.ds(0, NL - 1)], ar_ssem.at[3 + k, 1])
-        drain(gt_[k].at[pl.ds(0, NL - 1)], ar_ssem.at[3 + k, 2])
-        drain(gd_[k].at[pl.ds(0, ND - 1)], ar_ssem.at[3 + k, 3])
+        drain(gt_[k].at[pl.ds(0, 112)], ar_ssem.at[3 + k, 2])
+        with_block(k, lambda: drain(gda.at[pl.ds(0, NL - 1)], ar_ssem.at[3 + k, 3]))
     for j in range(NC):
         err_out(j).wait()
-    for o in books_out:
+    for o in outs:
         o.wait()
-    gram_out.wait()
 
 
 def refine(ids, fill, vectors, codes, centroids, codebooks):
@@ -504,7 +511,8 @@
     out_shape = [
         jax.ShapeDtypeStruct((SLOTS, 768), BF),
         jax.ShapeDtypeStruct((NC, ND, 16, 256), F32),
-        jax.ShapeDtypeStruct((768, 768), F32),
+        jax.ShapeDtypeStruct((NL, CW, CW), BF),
+        jax.ShapeDtypeStruct((6, CW, CW), BF),
     ]
     scratch = (
         [
@@ -513,32 +521,93 @@
             V((NC, NL, CAP, CW), BF), V((NC, NL, CAP, CW), BF),
             V((SLOTS, 768), BF), V((NC, MC, SLOTS), jnp.int32), V((96, 8, 256), F32),
             V((NC, SLOTS, CW), BF), V((NC, CW, SLOTS), BF), V((16, SLOTS), BF), V((4, 144, 256), F32),
-            V((NC, SLOTS, CW), BF), V((768, 768), F32),
+            V((NC, SLOTS, CW), BF),
         ]
         + [V((ND, sum_rows(g), 256), F32) for g in range(3)] * 2
         + [V((NL, 2 * w, 256), F32) for w in widths] * 2
         + [V((NL, w, 256), F32) for w in widths]
         + [V((ND, w, NL, 256), F32) for w in widths]
         + [V((ND, b, 16, CW), BF) for b in blocks] * 2
-        + [V((NL, 16, CW), BF) for _ in blocks] * 3
-        + [V((ND, n, 16, CW), BF) for n in (NL, 6)]
+        + [V((NL, 16, CW), BF) for _ in blocks] * 2
+        + [V((CW, CW), BF) for _ in blocks]
+        + [V((n, CW, CW), BF) for n in (NL, 6)]
         + [dma((3,)), dma((8,)), dma((3,)), dma, dma, dma, dma, dma((NC,)), dma((5, 4)), dma((5, 4))]
     )
     return pl.pallas_call(
         refine_kernel,
         out_shape=out_shape,
         in_specs=[pl.BlockSpec(memory_space=pltpu.VMEM), pl.BlockSpec(memory_space=pltpu.SMEM)] + [anyspace] * 4,
-        out_specs=[anyspace] * 3,
+        out_specs=[anyspace] * 4,
         scratch_shapes=scratch,
         compiler_params=pltpu.CompilerParams(
             collective_id=0, has_side_effects=True, vmem_limit_bytes=60 << 20),
     )(ids, fill, vectors, codes, centroids, codebooks)
 
 
+def finish_kernel(
+    err_in, books_in, ga_in, gb_in, err_out, books_out, gram_out, err, books, ga, gb, gram, in_sem, out_sem, gram_sem,
+):
+    parts = in_sem.shape[0] - 1
+    rows = err_in.shape[0] // parts
+
+    def pair(src, held, dst, i):
+        return pltpu.make_async_copy(src, held, in_sem.at[i]), pltpu.make_async_copy(held, dst, out_sem.at[i])
+
+    moves = []
+    for i in range(parts):
+        at = pl.ds(i * rows, rows)
+        moves.append(pair(err_in.at[at], err.at[at], err_out.at[at], i))
+    moves.append(pair(books_in, books, books_out, parts))
+    loads = [pltpu.make_async_copy(ga_in, ga, gram_sem.at[0]), pltpu.make_async_copy(gb_in, gb, gram_sem.at[1])]
+    for c in loads:
+        c.start()
+    for first, _ in moves:
+        first.start()
+    for c in loads:
+        c.wait()
+    for j in range(NC):
+        for i in range(j + 1):
+            block = (ga[block_of(j, i)] if j < NC - 1 else gb[i]).astype(F32)
+            jr, ir = slice(j * CW, (j + 1) * CW), slice(i * CW, (i + 1) * CW)
+            gram[jr, ir] = block
+            if i < j:
+                gram[ir, jr] = block.T
+    out = pltpu.make_async_copy(gram, gram_out, gram_sem.at[0])
+    out.start()
+    for first, second in moves:
+        first.wait()
+        second.start()
+    for _, second in moves:
+        second.wait()
+    out.wait()
+
+
+def finish(err, books, ga, gb):
+    anyspace = pl.BlockSpec(memory_space=pl.ANY)
+    dma = pltpu.SemaphoreType.DMA
+    return pl.pallas_call(
+        finish_kernel,
+        out_shape=[
+            jax.ShapeDtypeStruct(err.shape, BF),
+            jax.ShapeDtypeStruct(books.shape, F32),
+            jax.ShapeDtypeStruct((768, 768), F32),
+        ],
+        in_specs=[anyspace] * 4,
+        out_specs=[anyspace] * 3,
+        scratch_shapes=[
+            pltpu.VMEM(err.shape, BF), pltpu.VMEM(books.shape, F32),
+            pltpu.VMEM(ga.shape, BF), pltpu.VMEM(gb.shape, BF), pltpu.VMEM((768, 768), F32),
+            dma((9,)), dma((9,)), dma((2,)),
+        ],
+        compiler_params=pltpu.CompilerParams(vmem_limit_bytes=60 << 20),
+    )(err, books, ga, gb)
+
+
 def local(vectors, list_ids, codes, fill_counts, centroids, codebooks):
     codes_t = codes.T.reshape(NC, MC, SLOTS)
-    err, books, gram = refine(
+    err, books, ga, gb = refine(
         list_ids.reshape(NL, 1, CAP), fill_counts, vectors, codes_t, centroids, codebooks)
+    err, books, gram = finish(err, books, ga, gb)
     return err, books.reshape(96, 8, 256), gram
 
 

time: 111 us -> 98.5 us (0.89)
  Pallas kernels: 104 us -> 97.7 us
  local copies, waits for them, and re-layouts: 6.2 us -> 0 us
    pallas_call x1, Pallas kernels: 104 us -> 92.6 us  [refine(): pl.pallas_call(refine_kernel, out_shape=out_shape, in_specs=[pl.BlockSpec...]
    unnamed x7 -> x0, local copies, waits for them, and re-layouts: 6.2 us -> none
    pallas_call x0 -> x1, Pallas kernels: none -> 5.1 us  [finish(): pl.pallas_call(finish_kernel, out_shape=[jax.ShapeDtypeStruct(err.shape,...]
where the time goes in v3:
time: 98.5 us; the launch traced here: 98.3 us
  Pallas kernels  97.7 us (99%)
    pallas_call x1, Pallas kernels, refine(): pl.pallas_call(refine_kernel, out_shape=out_shape, in_specs=[pl.BlockSpec...  92.6 us
    pallas_call x1, Pallas kernels, finish(): pl.pallas_call(finish_kernel, out_shape=[jax.ShapeDtypeStruct(err.shape,...  5.1 us

profile of v3, /device:TPU:1, one launch (start us, length us, event | category | flops | bytes accessed | tf_op | source)
XLA Modules:
  0.0 98.3 jit_solution(11278266040486875856)
XLA Ops:
  0.6 92.6 %shard_map.85 = (bf16[2048,768]{1,0:T(8,128)(2,1)}, f32[6,8,16,256]{3,2,1,0:T(8,128)}, bf16[16,128,128]{2,1,0:T(8,128)(2,1)}, bf16[6,128,128]{2,1,0:T(8,128)(2,1)}) custom-call(s32[16,1,128]{2,1,0:T(1,128)} %bitcast.6, s32[1,16]{1,0:T(1,128)} %fill_ref.1, bf16[2048,768]{1,0:T(8,128)(2,1)} %vec_hbm.1, s32[6,16,2048]{2,1,0:T(8,128)} %bitcast.5, ...), custom_call_target="tpu_custom_call" | custom-call | tf_op jit(solution)/shard_map/pallas_call | solution.py:536
  93.2 5.1 %shard_map.86 = (bf16[2048,768]{1,0:T(8,128)(2,1)}, f32[6,8,16,256]{3,2,1,0:T(8,128)}, f32[768,768]{1,0:T(8,128)}) custom-call(bf16[2048,768]{1,0:T(8,128)(2,1)} %get-tuple-element.10.err_in, f32[6,8,16,256]{3,2,1,0:T(8,128)} %get-tuple-element.11.books_in, bf16[16,128,128]{2,1,0:T(8,128)(2,1)} %get-tuple-element.12.ga_in, ...), custom_call_target="tpu_custom_call" | custom-call | tf_op jit(solution)/shard_map/pallas_call | solution.py:588

commit v4 on v3

--- a/solution.py
+++ b/solution.py
@@ -254,12 +254,12 @@
                 for q in range(ND):
                     buf[q, first + i + k] = block[q * 16:q * 16 + 16, k * CW:(k + 1) * CW].astype(BF)
 
-    def start_dp(a, src, dst):
+    def start_dp(a, src, dst, part):
         def one(s, c):
             q = dp_peer(s)
             pltpu.make_async_remote_copy(
-                src_ref=src.at[q], dst_ref=dst.at[dp], send_sem=ar_ssem.at[a, 0], recv_sem=ar_rsem.at[a, 0],
-                device_id={"dp": q}, device_id_type=MESH).start()
+                src_ref=src.at[q, part], dst_ref=dst.at[dp, part], send_sem=ar_ssem.at[a, 0],
+                recv_sem=ar_rsem.at[a, 0], device_id={"dp": q}, device_id_type=MESH).start()
             return c
 
         lax.fori_loop(1, ND, one, 0)
@@ -294,8 +294,8 @@
 
     recv_sums, ls, lr, ag, ad = (dr0, dr1, dr2), (ls0, ls1, ls2), (lr0, lr1, lr2), (as0, as1, as2), (ad0, ad1, ad2)
 
-    def sums_1(g):
-        start_dp(g, send_sums[g], recv_sums[g])
+    def sums_1(g, u):
+        start_dp(g, send_sums[g], recv_sums[g], pl.ds(u * 24, 24))
 
     def sums_2(g):
         src, dst, width = send_sums[g], recv_sums[g], len(GROUPS[g])
@@ -336,8 +336,8 @@
 
     gs_, gr_, gl_, gm_, gt_, gd_ = (gsa, gsb), (gra, grb), (gla, glb), (gma, gmb), (gta, gtb), (gda, gdb)
 
-    def gram_1(k):
-        start_dp(3 + k, gs_[k], gr_[k])
+    def gram_1(k, first, count):
+        start_dp(3 + k, gs_[k], gr_[k], pl.ds(first, count))
 
     def gram_2(k):
         drain(gr_[k].at[pl.ds(0, ND - 1)], ar_rsem.at[3 + k, 0])
@@ -440,24 +440,27 @@
 
     def gram_early(j):
         gram_chunk(gsa, j, block_of(j, 0))
+        gram_1(0, block_of(j, 0), j + 1)
 
     chunk(0, 0, 0)
+    sums_1(0, 0)
     gram_early(0)
     chunk(0, 1, 1)
-    sums_1(0)
+    sums_1(0, 1)
     gram_early(1)
     chunk(1, 0, 2)
+    sums_1(1, 0)
     gram_early(2)
     chunk(1, 1, 3, sums_2)
-    sums_1(1)
+    sums_1(1, 1)
     gram_early(3)
     chunk(2, 0, 4, sums_3)
+    sums_1(2, 0)
     gram_early(4)
-    gram_1(0)
     chunk(2, 1, 5, lambda g: (sums_4(0), sums_2(1)))
-    sums_1(2)
+    sums_1(2, 1)
     gram_chunk(gsb, NC - 1, 0)
-    gram_1(1)
+    gram_1(1, 0, NC)
     gram_2(0)
     sums_3(1)
     sums_2(2)

time: 98.5 us -> 94.9 us (0.963)
  Pallas kernels: 97.7 us -> 93.9 us
    pallas_call x1, Pallas kernels: 92.6 us -> 88.8 us  [refine(): pl.pallas_call(refine_kernel, out_shape=out_shape, in_specs=[pl.BlockSpec...]
where the time goes in v4:
time: 94.9 us; the launch traced here: 94.5 us
  Pallas kernels  93.9 us (99%)
    pallas_call x1, Pallas kernels, refine(): pl.pallas_call(refine_kernel, out_shape=out_shape, in_specs=[pl.BlockSpec...  88.8 us
    pallas_call x1, Pallas kernels, finish(): pl.pallas_call(finish_kernel, out_shape=[jax.ShapeDtypeStruct(err.shape,...  5.1 us

profile of v4, /device:TPU:1, one launch (start us, length us, event | category | flops | bytes accessed | tf_op | source)
XLA Modules:
  0.0 94.5 jit_solution(16715482292711003888)
XLA Ops:
  0.6 88.8 %shard_map.85 = (bf16[2048,768]{1,0:T(8,128)(2,1)}, f32[6,8,16,256]{3,2,1,0:T(8,128)}, bf16[16,128,128]{2,1,0:T(8,128)(2,1)}, bf16[6,128,128]{2,1,0:T(8,128)(2,1)}) custom-call(s32[16,1,128]{2,1,0:T(1,128)} %bitcast.6, s32[1,16]{1,0:T(1,128)} %fill_ref.1, bf16[2048,768]{1,0:T(8,128)(2,1)} %vec_hbm.1, s32[6,16,2048]{2,1,0:T(8,128)} %bitcast.5, ...), custom_call_target="tpu_custom_call" | custom-call | tf_op jit(solution)/shard_map/pallas_call | solution.py:539
  89.4 5.1 %shard_map.86 = (bf16[2048,768]{1,0:T(8,128)(2,1)}, f32[6,8,16,256]{3,2,1,0:T(8,128)}, f32[768,768]{1,0:T(8,128)}) custom-call(bf16[2048,768]{1,0:T(8,128)(2,1)} %get-tuple-element.10.err_in, f32[6,8,16,256]{3,2,1,0:T(8,128)} %get-tuple-element.11.books_in, bf16[16,128,128]{2,1,0:T(8,128)(2,1)} %get-tuple-element.12.ga_in, ...), custom_call_target="tpu_custom_call" | custom-call | tf_op jit(solution)/shard_map/pallas_call | solution.py:591

commit v5 on v4

--- a/solution.py
+++ b/solution.py
@@ -48,10 +48,11 @@
     my_y, my_z = me // 4, me % 4
 
     def list_peer(s):
-        return lax.rem(my_y + s // 4, 4) * 4 + lax.rem(my_z + s % 4, 4)
+        t = lax.rem(s * 7, NL)
+        return lax.rem(my_y + t // 4, 4) * 4 + lax.rem(my_z + t % 4, 4)
 
     def dp_peer(s):
-        return lax.rem(dp + s, ND)
+        return lax.rem(dp + lax.rem(s + 2, ND - 1) + 1, ND)
 
     n_cent = cent_sem.shape[0]
     cent_rows = cbuf.shape[0] // n_cent

time: 94.9 us -> 93.8 us (0.988)
  the two profiles are of different devices: /device:TPU:1 before, /device:TPU:16 now
where the time goes in v5:
time: 93.8 us; the launch traced here: 93.6 us
  Pallas kernels  93 us (99%)
    pallas_call x1, Pallas kernels, refine(): pl.pallas_call(refine_kernel, out_shape=out_shape, in_specs=[pl.BlockSpec...  87.9 us
    pallas_call x1, Pallas kernels, finish(): pl.pallas_call(finish_kernel, out_shape=[jax.ShapeDtypeStruct(err.shape,...  5.1 us

profile of v5, /device:TPU:16, one launch (start us, length us, event | category | flops | bytes accessed | tf_op | source)
XLA Modules:
  0.0 93.6 jit_solution(5832308529246656650)
XLA Ops:
  0.6 87.9 %shard_map.85 = (bf16[2048,768]{1,0:T(8,128)(2,1)}, f32[6,8,16,256]{3,2,1,0:T(8,128)}, bf16[16,128,128]{2,1,0:T(8,128)(2,1)}, bf16[6,128,128]{2,1,0:T(8,128)(2,1)}) custom-call(s32[16,1,128]{2,1,0:T(1,128)} %bitcast.6, s32[1,16]{1,0:T(1,128)} %fill_ref.1, bf16[2048,768]{1,0:T(8,128)(2,1)} %vec_hbm.1, s32[6,16,2048]{2,1,0:T(8,128)} %bitcast.5, ...), custom_call_target="tpu_custom_call" | custom-call | tf_op jit(solution)/shard_map/pallas_call | solution.py:540
  88.5 5.1 %shard_map.86 = (bf16[2048,768]{1,0:T(8,128)(2,1)}, f32[6,8,16,256]{3,2,1,0:T(8,128)}, f32[768,768]{1,0:T(8,128)}) custom-call(bf16[2048,768]{1,0:T(8,128)(2,1)} %get-tuple-element.10.err_in, f32[6,8,16,256]{3,2,1,0:T(8,128)} %get-tuple-element.11.books_in, bf16[16,128,128]{2,1,0:T(8,128)(2,1)} %get-tuple-element.12.ga_in, ...), custom_call_target="tpu_custom_call" | custom-call | tf_op jit(solution)/shard_map/pallas_call | solution.py:592

commit v6 on v5

--- a/solution.py
+++ b/solution.py
@@ -91,8 +91,8 @@
         return c
 
 
-    table_rows = table.reshape(4096 * 8, 128)
-    gathered_rows = gbuf.reshape(32 * 8, 128)
+    table_rows = table.reshape(4104 * 8, 128)
+    gathered_rows = gbuf.reshape(40 * 8, 128)
 
     def build(b, c):
         cent_copy(b).wait()
@@ -452,7 +452,8 @@
     chunk(1, 0, 2)
     sums_1(1, 0)
     gram_early(2)
-    chunk(1, 1, 3, sums_2)
+    sums_2(0)
+    chunk(1, 1, 3)
     sums_1(1, 1)
     gram_early(3)
     chunk(2, 0, 4, sums_3)
@@ -521,7 +522,7 @@
     scratch = (
         [
             V((NL, 1, CAP), jnp.int32), pltpu.SMEM((NL, 1, CAP), jnp.int32),
-            V((4096, 8, 128), F32), V((4096, 768), BF), V((32, 8, 128), F32),
+            V((4104, 8, 128), F32), V((4096, 768), BF), V((40, 8, 128), F32),
             V((NC, NL, CAP, CW), BF), V((NC, NL, CAP, CW), BF),
             V((SLOTS, 768), BF), V((NC, MC, SLOTS), jnp.int32), V((96, 8, 256), F32),
             V((NC, SLOTS, CW), BF), V((NC, CW, SLOTS), BF), V((16, SLOTS), BF), V((4, 144, 256), F32),

time: 93.8 us -> 93.8 us (level)
  the two profiles are of different devices: /device:TPU:16 before, /device:TPU:1 now
where the time goes in v6:
time: 93.8 us; the launch traced here: 92.1 us
  Pallas kernels  91.5 us (98%)
    pallas_call x1, Pallas kernels, refine(): pl.pallas_call(refine_kernel, out_shape=out_shape, in_specs=[pl.BlockSpec...  86.4 us
    pallas_call x1, Pallas kernels, finish(): pl.pallas_call(finish_kernel, out_shape=[jax.ShapeDtypeStruct(err.shape,...  5.1 us

profile of v6, /device:TPU:1, one launch (start us, length us, event | category | flops | bytes accessed | tf_op | source)
XLA Modules:
  0.0 92.1 jit_solution(14508337305100943944)
XLA Ops:
  0.6 86.4 %shard_map.85 = (bf16[2048,768]{1,0:T(8,128)(2,1)}, f32[6,8,16,256]{3,2,1,0:T(8,128)}, bf16[16,128,128]{2,1,0:T(8,128)(2,1)}, bf16[6,128,128]{2,1,0:T(8,128)(2,1)}) custom-call(s32[16,1,128]{2,1,0:T(1,128)} %bitcast.6, s32[1,16]{1,0:T(1,128)} %fill_ref.1, bf16[2048,768]{1,0:T(8,128)(2,1)} %vec_hbm.1, s32[6,16,2048]{2,1,0:T(8,128)} %bitcast.5, ...), custom_call_target="tpu_custom_call" | custom-call | tf_op jit(solution)/shard_map/pallas_call | solution.py:541
  87.0 5.1 %shard_map.86 = (bf16[2048,768]{1,0:T(8,128)(2,1)}, f32[6,8,16,256]{3,2,1,0:T(8,128)}, f32[768,768]{1,0:T(8,128)}) custom-call(bf16[2048,768]{1,0:T(8,128)(2,1)} %get-tuple-element.10.err_in, f32[6,8,16,256]{3,2,1,0:T(8,128)} %get-tuple-element.11.books_in, bf16[16,128,128]{2,1,0:T(8,128)(2,1)} %get-tuple-element.12.ga_in, ...), custom_call_target="tpu_custom_call" | custom-call | tf_op jit(solution)/shard_map/pallas_call | solution.py:593
